TPU v7x, 32 devices: a whole 2x2x4 slice. The times are simulated.
32 devices in a mesh: group: 2 (over y), seq: 8 (over z, x), mp: 2 (over core).
Axes of the slice: x: 2, y: 2, z: 4, core: 2. Of those that a mesh axis runs over, the one named last changes fastest.
Arguments:
- student_hidden: bfloat16 [2, 1024, 3072], P('group', 'seq', 'mp'), may hold values from -6 to 6
- student_cond: float32 [2, 3072], P(None, 'seq'), may hold values from -6 to 6
- student_mod: bfloat16 [3072, 2, 3072], P('seq', 'group', 'mp'), may hold values from -0.109375 to 0.109375
- student_out: bfloat16 [3072, 64], P('mp'), may hold values from -0.109375 to 0.109375
- timestep: int32 [2], P('group'), may hold values from 0 to 999
- noise: bfloat16 [2, 1024, 64], P('group', 'seq'), may hold values from -6 to 6
- teacher_embed: bfloat16 [64, 3072], P(None, 'mp'), may hold values from -0.75 to 0.75
- teacher_mod: bfloat16 [256, 2, 3072], P(None, None, 'mp'), may hold values from -0.375 to 0.375
- up_weight: bfloat16 [3072, 6144], P('seq', 'mp'), may hold values from -0.109375 to 0.109375
- down_weight: bfloat16 [6144, 3072], P('mp', 'seq'), may hold values from -0.078125 to 0.078125
- head_proj: bfloat16 [4, 3072, 128], P(None, 'mp'), may hold values from -0.109375 to 0.109375
- head_kernel: float32 [4, 3, 3, 128], replicated, may hold values from -3 to 3
- head_out: float32 [4, 128], replicated, may hold values from -2 to 2
- disc_layer: int32 [2, 4], P('group'), may hold values from 0 to 1, as said below
Outputs:
- latents: bfloat16 [2, 1024, 64], P('group', 'seq')
- logits: float32 [2, 4, 1024], P('group', None, 'seq')
- latent_grad: float32 [2, 1024, 64], P('group', 'seq')
Inputs may be any that keep to these rules, and one draw needn't show every extreme that they name: `disc_layer`: for every sample, exactly half of the 4 heads read layer 0 and the other half layer 1, in an order drawn afresh.
All inputs are finite; a program needn't handle non-finite values.
Results may differ from a plain program's by a relative error of at most 0.029.
Values may be sent and summed in bfloat16 or wider, within the bound.
A program may use at most 128 MiB of HBM per device.

v0:
```python
import math

import jax
import jax.numpy as jnp
from jax import lax
from jax.sharding import PartitionSpec as P

GRID_W = 64


EPSILON = 1e-06
GELU_COEF = 0.7978845608028654


def extended(value, sides, width):
    for axis, dim in sides:
        count, length = (lax.axis_size(axis), value.shape[dim])
        up = [(i, (i + 1) % count) for i in range(count - 1)]
        down = [(j, i) for i, j in up]
        last = lax.slice_in_dim(value, length - width, length, axis=dim)
        first = lax.slice_in_dim(value, 0, width, axis=dim)
        before = lax.ppermute(last, axis, up)
        after = lax.ppermute(first, axis, down)
        value = jnp.concatenate([before, value, after], axis=dim)
    return value


def gelu_tanh(values):
    inner = GELU_COEF * (values + 0.044715 * values * values * values)
    return 0.5 * values * (1.0 + jnp.tanh(inner))


def gelu_slope(values):
    inner = GELU_COEF * (values + 0.044715 * values * values * values)
    tangent = jnp.tanh(inner)
    return 0.5 * (1.0 + tangent) + 0.5 * values * (1.0 - tangent * tangent) * GELU_COEF * (
        1.0 + 3.0 * 0.044715 * values * values
    )


def time_features(timestep, width):
    half_width = width // 2
    index = jnp.arange(half_width, dtype=jnp.float32)
    freqs = jnp.exp(-math.log(10000.0) * index / half_width)
    angles = timestep.astype(jnp.float32)[:, None] * freqs[None, :]
    return jnp.concatenate([jnp.cos(angles), jnp.sin(angles)], axis=-1)


def forward_conv(grid, kernel):
    padded = extended(grid.astype(jnp.bfloat16), (("seq", 2),), 1).astype(grid.dtype)
    padded = jnp.pad(padded, ((0, 0), (0, 0), (0, 0), (1, 1), (0, 0)))
    grid_rows = grid.shape[2]
    grid_cols = grid.shape[3]
    summed = jnp.zeros(grid.shape, jnp.float32)
    for row_off in range(3):
        for col_off in range(3):
            summed = (
                summed
                + kernel[:, row_off, col_off][None, :, None, None, :]
                * padded[:, :, row_off : row_off + grid_rows, col_off : col_off + grid_cols, :]
            )
    return summed


def backward_conv(grid, kernel):
    padded = extended(grid.astype(jnp.bfloat16), (("seq", 2),), 1).astype(grid.dtype)
    padded = jnp.pad(padded, ((0, 0), (0, 0), (0, 0), (1, 1), (0, 0)))
    grid_rows = grid.shape[2]
    grid_cols = grid.shape[3]
    summed = jnp.zeros(grid.shape, jnp.float32)
    for row_off in range(3):
        for col_off in range(3):
            summed = (
                summed
                + kernel[:, row_off, col_off][None, :, None, None, :]
                * padded[
                    :,
                    :,
                    2 - row_off : 2 - row_off + grid_rows,
                    2 - col_off : 2 - col_off + grid_cols,
                    :,
                ]
            )
    return summed


def per_device(
    student_hidden,
    student_cond,
    student_mod,
    student_out,
    timestep,
    noise,
    teacher_embed,
    teacher_mod,
    up_weight,
    down_weight,
    head_proj,
    head_kernel,
    head_out,
    disc_layer,
):
    highest = lax.Precision.HIGHEST
    samples = student_hidden.shape[0]
    model_width = student_hidden.shape[2] * lax.axis_size("mp")
    hidden = student_hidden.astype(jnp.float32)
    first_sum, square_sum = lax.psum((jnp.sum(hidden, -1), jnp.sum(hidden * hidden, -1)), "mp")
    tok_mean = (first_sum / model_width)[..., None]
    tok_var = (square_sum / model_width)[..., None] - tok_mean * tok_mean
    half_mod = jnp.einsum(
        "sk,kjd->sjd", student_cond, student_mod.astype(jnp.float32), precision=highest
    )
    half_mod = lax.psum(half_mod, "seq")
    halves_all = lax.all_gather(half_mod, "group", axis=1, tiled=True)
    own_mod = lax.dynamic_slice_in_dim(halves_all, lax.axis_index("group") * samples, samples, 0)
    normed = (
        (hidden - tok_mean) * lax.rsqrt(tok_var + EPSILON) * (1.0 + own_mod[:, 1:2])
        + own_mod[:, 0:1]
    ).astype(jnp.bfloat16)
    latent_terms = jnp.einsum(
        "std,dc->stc", normed, student_out, preferred_element_type=jnp.float32
    )
    latents = lax.psum(latent_terms.astype(jnp.bfloat16), "mp")
    level = timestep.astype(jnp.float32) / 1000.0
    retain = (1.0 - level)[:, None, None]
    noised = (
        retain * latents.astype(jnp.float32) + level[:, None, None] * noise.astype(jnp.float32)
    ).astype(jnp.bfloat16)
    embedded = jnp.einsum(
        "stc,cd->std", noised, teacher_embed, preferred_element_type=jnp.float32
    ).astype(jnp.bfloat16)
    tmod = jnp.einsum(
        "sf,fjd->sjd",
        time_features(timestep, teacher_mod.shape[0]),
        teacher_mod.astype(jnp.float32),
        precision=highest,
    )
    emb_f = embedded.astype(jnp.float32)
    sum_t, square_t = lax.psum((jnp.sum(emb_f, -1), jnp.sum(emb_f * emb_f, -1)), "mp")
    mean_t = (sum_t / model_width)[..., None]
    var_t = (square_t / model_width)[..., None] - mean_t * mean_t
    inv_std = lax.rsqrt(var_t + EPSILON)
    centered = (emb_f - mean_t) * inv_std
    mod_gain = 1.0 + tmod[:, 1:2]
    modulated = (centered * mod_gain + tmod[:, 0:1]).astype(jnp.bfloat16)
    full_input = lax.all_gather(modulated, "mp", axis=2, tiled=True)
    up_full = lax.all_gather(up_weight, "seq", axis=0, tiled=True)
    preact = jnp.einsum("std,df->stf", full_input, up_full, preferred_element_type=jnp.float32)
    activated = gelu_tanh(preact).astype(jnp.bfloat16)
    down_full = lax.all_gather(down_weight, "seq", axis=1, tiled=True)
    out_terms = jnp.einsum("stf,fd->std", activated, down_full, preferred_element_type=jnp.float32)
    block_out = (
        emb_f
        + lax.psum_scatter(
            out_terms.astype(jnp.bfloat16), "mp", scatter_dimension=2, tiled=True
        ).astype(jnp.float32)
    ).astype(jnp.bfloat16)
    head_count = disc_layer.shape[1]
    layer_pick = disc_layer == 1
    features = jnp.where(layer_pick[:, :, None, None], block_out[:, None], embedded[:, None])
    proj_terms = jnp.einsum(
        "sktd,kdc->sktc", features, head_proj, preferred_element_type=jnp.float32
    )
    local_tokens = features.shape[2]
    grid_rows = local_tokens // GRID_W
    projected = lax.psum(proj_terms.astype(jnp.bfloat16), "mp").astype(jnp.float32)
    channels = projected.shape[3]
    grid = projected.reshape(samples, head_count, grid_rows, GRID_W, channels)
    conv_field = forward_conv(grid, head_kernel)
    gating = jax.nn.sigmoid(conv_field)
    out_scale = head_out[None, :, None, None, :]
    logit_terms = jnp.sum(conv_field * gating * out_scale, -1).reshape(
        samples, head_count, local_tokens
    )
    slope_grad = -out_scale * gating * (1.0 + conv_field * (1.0 - gating))
    field_grad = (
        backward_conv(slope_grad, head_kernel)
        .reshape(samples, head_count, local_tokens, channels)
        .astype(jnp.bfloat16)
    )
    head_grads = jnp.einsum(
        "sktc,kdc->sktd", field_grad, head_proj, preferred_element_type=jnp.float32
    )
    pick_f = layer_pick.astype(jnp.float32)[:, :, None, None]
    grad_out = jnp.sum(pick_f * head_grads, 1)
    grad_embed = jnp.sum((1.0 - pick_f) * head_grads, 1)
    full_grad = lax.all_gather(grad_out.astype(jnp.bfloat16), "mp", axis=2, tiled=True)
    hidden_grad = jnp.einsum(
        "std,fd->stf", full_grad, down_full, preferred_element_type=jnp.float32
    )
    preact_grad = (hidden_grad * gelu_slope(preact)).astype(jnp.bfloat16)
    input_terms = jnp.einsum(
        "stf,df->std", preact_grad, up_full, preferred_element_type=jnp.float32
    )
    input_grad = lax.psum_scatter(
        input_terms.astype(jnp.bfloat16), "mp", scatter_dimension=2, tiled=True
    ).astype(jnp.float32)
    scaled = input_grad * mod_gain
    sum_one, sum_two = lax.psum((jnp.sum(scaled, -1), jnp.sum(scaled * centered, -1)), "mp")
    embed_grad = (
        (
            scaled
            - (sum_one / model_width)[..., None]
            - centered * (sum_two / model_width)[..., None]
        )
        * inv_std
        + grad_out
        + grad_embed
    )
    latent_terms_back = jnp.einsum(
        "std,cd->stc",
        embed_grad.astype(jnp.bfloat16),
        teacher_embed,
        preferred_element_type=jnp.float32,
    )
    latent_grad = retain * lax.psum(latent_terms_back.astype(jnp.bfloat16), "mp").astype(
        jnp.float32
    )
    return (latents, logit_terms, latent_grad)


def solution(mesh):
    return jax.shard_map(
        per_device,
        mesh=mesh,
        in_specs=(
            P("group", "seq", "mp"),
            P(None, "seq"),
            P("seq", "group", "mp"),
            P("mp", None),
            P("group"),
            P("group", "seq", None),
            P(None, "mp"),
            P(None, None, "mp"),
            P("seq", "mp"),
            P("mp", "seq"),
            P(None, "mp", None),
            P(),
            P(),
            P("group", None),
        ),
        out_specs=(P("group", "seq", None), P("group", None, "seq"), P("group", "seq", None)),
        check_vma=False,
    )
```

profile of v0, /device:TPU:0, one launch (start us, length us, event | category | flops | bytes accessed | tf_op | source)
XLA Modules:
  0.0 860.7 jit_solution(15121011293873463396)
XLA Ops:
  10.4 2.6 all-reduce.4
  13.0 1.8 convolution_bitcast_fusion.1
  14.8 64.6 %psum.72 = f32[2,1,1536]{2,0,1:T(2,128)S(1)} all-reduce(f32[2,1,1536]{2,0,1:T(2,128)S(1)} %convolution_bitcast_fusion.1), channel_id=1, replica_groups=mesh['group'=2,'seq'=8,'mp'=2] {'seq'}, use_global_device_ids=true, to_apply=%region_4.0 | all-reduce | flops 3072 | bytes 24576 | tf_op jit(solution)/shard_map/psum | solution.py:113
  79.5 4.4 all_gather.15
  84.3 3.4 psum.73
  88.1 2.5 all-reduce.3
  90.9 2.4 all-gather
  93.3 282.7 %all-gather.4.cloned.1.call-done = bf16[3072,3072]{1,0:T(8,128)(2,1)} async-done(((bf16[384,3072]{1,0:T(8,128)(2,1)}), bf16[3072,3072]{1,0:T(8,128)(2,1)}) %all-gather.4.cloned.1.call-update) | async-done | bytes 18874384 | tf_op jit(solution)/shard_map/all_gather | solution.py:147
  376.0 10.1 %fusion.110 = f32[128,3072]{1,0:T(8,128)} fusion(bf16[128,3072]{1,0:T(8,128)(2,1)S(1)} %all-gather, bf16[3072,3072]{1,0:T(8,128)(2,1)} %all-gather.4.cloned.1.call-done), kind=kOutput, calls=%fused_computation.175 | convolution fusion | flops 2415919104 | bytes 21233664 | tf_op jit(solution)/shard_map/std,df->stf/dot_general | solution.py:148
  386.1 353.9 %all-gather.6.cloned.1.call-done = bf16[3072,3072]{1,0:T(8,128)(2,1)} async-done(((bf16[3072,384]{1,0:T(8,128)(2,1)}), bf16[3072,3072]{1,0:T(8,128)(2,1)}) %all-gather.6.cloned.1.call-update) | async-done | bytes 18874384 | tf_op jit(solution)/shard_map/all_gather | solution.py:150
  740.0 10.5 %fusion.1 = bf16[1,128,3072]{2,1,0:T(8,128)(2,1)} fusion(bf16[3072,3072]{1,0:T(8,128)(2,1)} %all-gather.6.cloned.1.call-done, f32[128,3072]{1,0:T(8,128)} %fusion.110), kind=kOutput, calls=%fused_computation.4 | convolution fusion | flops 2419851264 | bytes 21233664 | tf_op jit(solution)/shard_map/stf,fd->std/dot_general | solution.py:151
  750.6 8.3 reduce-scatter.3.cloned.1.call-done
  758.9 1.1 fusion.49
  760.1 1.3 fusion.14
  761.4 19.2 %all-reduce.7.cloned.1.call-done = bf16[1,4,2,64,128]{4,3,2,1,0:T(8,128)(2,1)} async-done(((bf16[1,4,2,64,128]{4,3,2,1,0:T(8,128)(2,1)}), bf16[1,4,2,64,128]{4,3,2,1,0:T(8,128)(2,1)}) %all-reduce.7.cloned.1.call-update) | async-done | bytes 131088 | tf_op jit(solution)/shard_map/psum | solution.py:166
  780.6 0.9 fusion.109
  781.5 3.6 collective-permute-start
  785.1 1.3 collective-permute-start.1
  787.0 4.3 collective-permute-done.1
  791.3 0.9 maximum_convert_fusion
  792.6 4.3 collective-permute-start.2
  796.9 1.3 collective-permute-start.3
  798.8 4.3 collective-permute-done.3
  803.4 1.6 multiply_reduce_fusion.1
  805.0 2.7 all_gather.19
  807.7 14.7 %fusion = bf16[128,3072]{1,0:T(8,128)(2,1)} fusion(bf16[3072,3072]{1,0:T(8,128)(2,1)} %all-gather.6.cloned.1.call-done, f32[128,3072]{1,0:T(8,128)} %fusion.110, bf16[1,128,3072]{2,1,0:T(8,128)(2,1)} %all_gather.19), kind=kOutput, calls=%fused_computation.3 | convolution fusion | flops 2423390208 | bytes 22020096 | tf_op jit(solution)/shard_map/std,fd->stf/dot_general | solution.py:188
  822.4 13.9 %fusion.2 = bf16[1,128,3072]{2,1,0:T(8,128)(2,1)} fusion(bf16[128,3072]{1,0:T(8,128)(2,1)} %fusion, bf16[3072,3072]{1,0:T(8,128)(2,1)} %all-gather.4.cloned.1.call-done), kind=kOutput, calls=%fused_computation.5 | convolution fusion | flops 2416312320 | bytes 20447232 | tf_op jit(solution)/shard_map/stf,df->std/dot_general | solution.py:192
  837.1 7.6 reduce-scatter.5.cloned.1.call-done
  844.6 1.3 fusion.42
  845.9 2.5 all-reduce.2
  848.4 1.7 fusion.18
  850.1 3.4 psum.79
  (62 shorter events, 7.1 us)
Async XLA Ops:
  7.2 752.9 %copy-start = (bf16[4,1536,128]{2,1,0:T(8,128)(2,1)S(1)}, bf16[4,1536,128]{2,1,0:T(8,128)(2,1)}, u32[]{:S(2)}) copy-start(bf16[4,1536,128]{2,1,0:T(8,128)(2,1)} %param.24) | copy-start | bytes 4718596
  7.2 368.8 %all-gather.4.cloned.1.call-start = ((), (), s32[]{:S(2)}) async-start(), calls=%async_computation.2 | async-start | bytes 21233664 | tf_op jit(solution)/shard_map/all_gather | solution.py:147
  7.9 1.5 copy-start.1
  7.9 2.3 copy-start.3
  7.9 732.1 %all-gather.6.cloned.1.call-start = ((), (), s32[]{:S(2)}) async-start(), calls=%async_computation.3 | async-start | bytes 21233664 | tf_op jit(solution)/shard_map/all_gather | solution.py:150
  8.7 4.3 copy-start.8
  8.7 750.3 %reduce-scatter.3.cloned.1.call-start = ((), (), s32[]{:S(2)}) async-start(), calls=%async_computation.4 | async-start | bytes 1179648 | tf_op jit(solution)/shard_map/reduce_scatter | solution.py:154
  10.2 73.8 %copy-start.9 = (bf16[1536,64]{0,1:T(8,128)(2,1)S(1)}, bf16[1536,64]{0,1:T(8,128)(2,1)}, u32[]{:S(2)}) copy-start(bf16[1536,64]{0,1:T(8,128)(2,1)} %param.17) | copy-start | bytes 589828
  10.2 77.5 %copy-start.2 = (bf16[64,1536]{1,0:T(8,128)(2,1)S(1)}, bf16[64,1536]{1,0:T(8,128)(2,1)}, u32[]{:S(2)}) copy-start(bf16[64,1536]{1,0:T(8,128)(2,1)} %param.20) | copy-start | bytes 589828
  10.2 77.5 %copy-start.6 = (bf16[1,128,64]{1,2,0:T(8,128)(2,1)S(1)}, bf16[1,128,64]{1,2,0:T(8,128)(2,1)}, u32[]{:S(2)}) copy-start(bf16[1,128,64]{1,2,0:T(8,128)(2,1)} %param.19) | copy-start | bytes 49156
  87.7 298.4 %copy-start.4 = (bf16[1,128,64]{1,2,0:T(8,128)(2,1)}, bf16[1,128,64]{1,2,0:T(8,128)(2,1)S(1)}, u32[]{:S(2)}) copy-start(bf16[1,128,64]{1,2,0:T(8,128)(2,1)S(1)} %psum.73) | copy-start | bytes 49156
  386.1 364.5 %copy-start.10 = (s32[1,4]{1,0:T(1,128)S(1)}, s32[1,4]{1,0:T(1,128)}, u32[]{:S(2)}) copy-start(s32[1,4]{1,0:T(1,128)} %param.27) | copy-start | bytes 52
  750.6 30.1 %all-reduce.7.cloned.1.call-start = ((), (), s32[]{:S(2)}) async-start(), calls=%async_computation.5 | async-start | bytes 262144 | tf_op jit(solution)/shard_map/psum | solution.py:166
  760.0 26.4 %copy-start.5 = (f32[4,3,3,128]{3,0,2,1:T(4,128)S(1)}, f32[4,3,3,128]{3,0,2,1:T(4,128)}, u32[]{:S(2)}) copy-start(f32[4,3,3,128]{3,0,2,1:T(4,128)} %param.25) | copy-start | bytes 55300
  760.1 26.4 %copy-start.7 = (f32[4,128]{1,0:T(4,128)S(1)}, f32[4,128]{1,0:T(4,128)}, u32[]{:S(2)}) copy-start(f32[4,128]{1,0:T(4,128)} %param.26) | copy-start | bytes 6148
  761.4 83.2 %reduce-scatter.5.cloned.1.call-start = ((), (), s32[]{:S(2)}) async-start(), calls=%async_computation.6 | async-start | bytes 1179648 | tf_op jit(solution)/shard_map/reduce_scatter | solution.py:195
  781.5 5.5 collective-permute-start
  785.1 6.2 collective-permute-start.1
  792.6 6.2 collective-permute-start.2
  796.9 6.2 collective-permute-start.3
Sparse Core Ops, SparseCore 0:
  9.6 366.3 all-gather.3
  377.5 362.4 all-gather.5
  750.7 8.2 reduce-scatter.2
  761.5 19.0 all-reduce.6
  836.4 8.2 reduce-scatter.4
where the time goes:
time: 861 us
  waiting for transfers between devices  683 us (79%)
  blocking collectives  88.4 us (10%)
  matrix products  57.1 us (7%)
  between operations  14.7 us (2%)
  starting transfers between devices  10.7 us (1%)
    all_gather x1, waiting for transfers between devices, per_device(): down_full = lax.all_gather(down_weight, 'seq', axis=1, tiled=True)  354 us
    all_gather x1, waiting for transfers between devices, per_device(): up_full = lax.all_gather(up_weight, 'seq', axis=0, tiled=True)  283 us
    psum x1, blocking collectives, per_device(): half_mod = lax.psum(half_mod, 'seq')  64.6 us
    psum x1, waiting for transfers between devices, per_device(): lax.psum(proj_terms.astype(jnp.bfloat16), 'mp').astype(jnp.float32)  19.2 us
  transfers between devices with their start and end apart: 9, of which 9 were waited for; matrix products, arithmetic and copies ran while one was open for 2% of the time, Pallas kernels for 0%

commit v1 on v0

v1 whole, which is shorter than its diff:
```python
import math

import jax
import jax.numpy as jnp
from jax import lax
from jax.sharding import PartitionSpec as P

GRID_W = 64


EPSILON = 1e-06
GELU_COEF = 0.7978845608028654


def gelu_tanh(values):
    inner = GELU_COEF * (values + 0.044715 * values * values * values)
    return 0.5 * values * (1.0 + jnp.tanh(inner))


def gelu_slope(values):
    inner = GELU_COEF * (values + 0.044715 * values * values * values)
    tangent = jnp.tanh(inner)
    return 0.5 * (1.0 + tangent) + 0.5 * values * (1.0 - tangent * tangent) * GELU_COEF * (
        1.0 + 3.0 * 0.044715 * values * values
    )


def time_features(timestep, width):
    half_width = width // 2
    index = jnp.arange(half_width, dtype=jnp.float32)
    freqs = jnp.exp(-math.log(10000.0) * index / half_width)
    angles = timestep.astype(jnp.float32)[:, None] * freqs[None, :]
    return jnp.concatenate([jnp.cos(angles), jnp.sin(angles)], axis=-1)


def shifted(grid, offset):
    zero = jnp.zeros_like(grid[:, :, :1])
    if offset == -1:
        return jnp.concatenate([zero, grid[:, :, :-1]], axis=2)
    if offset == 1:
        return jnp.concatenate([grid[:, :, 1:], zero], axis=2)
    return grid


def conv_rows(grid, kernel, sign):
    rows = grid.shape[1] - 2
    total = None
    moved = {off: shifted(grid, off) for off in (-1, 0, 1)}
    for i in range(3):
        for j in range(3):
            row = 1 + sign * (i - 1)
            term = kernel[:, i, j][:, None, None, :] * moved[sign * (j - 1)][:, row : row + rows]
            total = term if total is None else total + term
    return total


def per_device(
    student_hidden,
    student_cond,
    student_mod,
    student_out,
    timestep,
    noise,
    teacher_embed,
    teacher_mod,
    up_weight,
    down_weight,
    head_proj,
    head_kernel,
    head_out,
    disc_layer,
):
    highest = lax.Precision.HIGHEST
    f32, bf16 = jnp.float32, jnp.bfloat16
    n_mp, n_seq = lax.axis_size("mp"), lax.axis_size("seq")
    seq = lax.axis_index("seq")
    tokens = student_hidden.shape[1]
    rows = tokens // GRID_W
    local_width = student_hidden.shape[2]
    width = local_width * n_mp
    latent_width = noise.shape[2]
    heads, _, channels = head_proj.shape
    picked = heads // 2

    reads = (disc_layer[0] == 1).astype(jnp.int32)
    order = jnp.arange(heads)
    rank = jnp.sum(jnp.where(order[None, :] < order[:, None], reads[None, :], 0), axis=1)
    slot_head = [
        jnp.sum(jnp.where((reads == 1) & (rank == j), jnp.arange(heads), 0)) for j in range(picked)
    ]
    one_hot = jnp.stack(
        [((reads == 1) & (rank == j)).astype(f32) for j in range(picked)], axis=1
    )

    embed_full = lax.all_gather(teacher_embed, "mp", axis=1, tiled=True)
    tmod = jnp.einsum(
        "f,fjd->jd",
        time_features(timestep, teacher_mod.shape[0])[0],
        teacher_mod.astype(f32),
        precision=highest,
    )
    tmod = lax.all_gather(tmod, "mp", axis=1, tiled=True)
    chunk = width // n_seq
    start = seq * chunk
    owner = start // local_width
    offset = start - owner * local_width
    own_proj = jnp.stack(
        [
            lax.dynamic_slice(head_proj, (slot_head[j], offset, 0), (1, chunk, channels))[0]
            for j in range(picked)
        ],
        axis=1,
    ).reshape(chunk, picked * channels)
    own_proj = jnp.where(lax.axis_index("mp") == owner, own_proj, jnp.zeros_like(own_proj))
    proj_chunk = lax.psum(own_proj, "mp")
    out_fold = lax.psum(
        jnp.dot(down_weight, proj_chunk, preferred_element_type=f32).astype(bf16), "seq"
    )
    embed_f = embed_full.astype(f32)
    embed_centered = embed_f - jnp.mean(embed_f, axis=1, keepdims=True)
    gram = jnp.einsum("cd,ed->ce", embed_centered, embed_centered, precision=highest)
    stacked = jnp.concatenate(
        [embed_centered * (1.0 + tmod[1:2]), tmod[0:1]], axis=0
    ).astype(bf16)
    stacked = lax.dynamic_slice_in_dim(stacked, start, chunk, 1)
    in_fold = lax.psum(
        jnp.dot(stacked, up_weight, preferred_element_type=f32).astype(bf16), "seq"
    )
    embed_proj = lax.psum(
        jnp.einsum("cd,kdh->kch", teacher_embed, head_proj, preferred_element_type=f32), "mp"
    )

    hidden = student_hidden[0].astype(f32)
    first_sum, square_sum = lax.psum((jnp.sum(hidden, -1), jnp.sum(hidden * hidden, -1)), "mp")
    tok_mean = (first_sum / width)[:, None]
    tok_var = (square_sum / width)[:, None] - tok_mean * tok_mean
    half_mod = jnp.einsum(
        "sk,kjd->sjd", student_cond, student_mod.astype(f32), precision=highest
    )
    half_mod = lax.psum(half_mod, "seq")
    halves_all = lax.all_gather(half_mod, "group", axis=1, tiled=True)
    own_mod = lax.dynamic_slice_in_dim(halves_all, lax.axis_index("group"), 1, 0)[0]
    normed = (
        (hidden - tok_mean) * lax.rsqrt(tok_var + EPSILON) * (1.0 + own_mod[1:2]) + own_mod[0:1]
    ).astype(bf16)
    latents = lax.psum(
        jnp.dot(normed, student_out, preferred_element_type=f32).astype(bf16), "mp"
    )
    level = timestep[0].astype(f32) / 1000.0
    retain = 1.0 - level
    noised = (retain * latents.astype(f32) + level * noise[0].astype(f32)).astype(bf16)

    halo = 2 * GRID_W
    ups = [(i, i + 1) for i in range(n_seq - 1)]
    downs = [(j, i) for i, j in ups]
    before = lax.ppermute(noised[tokens - halo :], "seq", ups)
    after = lax.ppermute(noised[:halo], "seq", downs)
    wide = jnp.concatenate([before, noised, after], axis=0)

    wide_f = wide.astype(f32)
    wide_gram = jnp.dot(wide_f, gram, precision=highest)
    var_t = jnp.sum(wide_f * wide_gram, -1, keepdims=True) / width
    inv_std = lax.rsqrt(var_t + EPSILON)
    up_fold = in_fold[:latent_width]
    bias = in_fold[latent_width:].astype(f32)
    preact = inv_std * jnp.dot(wide, up_fold, preferred_element_type=f32) + bias
    activated = gelu_tanh(preact).astype(bf16)
    block_terms = lax.psum(
        jnp.dot(activated, out_fold, preferred_element_type=f32).astype(bf16), "mp"
    ).astype(f32)
    projected = jnp.einsum("tc,kch->kth", wide_f, embed_proj, precision=highest)
    projected = projected + sum(
        one_hot[:, j][:, None, None]
        * block_terms[:, j * channels : (j + 1) * channels][None]
        for j in range(picked)
    )
    grid = projected.reshape(heads, rows + 4, GRID_W, channels)
    row_id = seq * rows - 2 + jnp.arange(rows + 4)
    inside = ((row_id >= 0) & (row_id < rows * n_seq)).astype(f32)[None, :, None, None]
    conv_field = conv_rows(grid * inside, head_kernel, 1)
    gating = jax.nn.sigmoid(conv_field)
    out_scale = head_out[:, None, None, :]
    logits = jnp.sum((conv_field * gating * out_scale)[:, 1 : rows + 1], -1).reshape(
        1, heads, tokens
    )
    slope_grad = -out_scale * gating * (1.0 + conv_field * (1.0 - gating)) * inside[:, 1:-1]
    field_grad = conv_rows(slope_grad, head_kernel, -1).reshape(heads, tokens, channels)
    field_grad = field_grad.astype(bf16)
    head_part = jnp.einsum("kth,kch->tc", field_grad.astype(f32), embed_proj, precision=highest)
    picked_grad = jnp.concatenate(
        [
            jnp.sum(field_grad * one_hot[:, j][:, None, None].astype(bf16), 0)
            for j in range(picked)
        ],
        axis=1,
    )
    hidden_grad = lax.dot_general(
        picked_grad, out_fold, (((1,), (1,)), ((), ())), preferred_element_type=f32
    )
    own = slice(halo, halo + tokens)
    preact_grad = (hidden_grad * gelu_slope(preact[own])).astype(bf16)
    scaled_back = lax.psum(
        lax.dot_general(
            preact_grad, up_fold, (((1,), (1,)), ((), ())), preferred_element_type=f32
        ),
        "mp",
    )
    noised_f, own_inv = wide_f[own], inv_std[own]
    along = jnp.sum(noised_f * scaled_back, -1, keepdims=True) / width
    latent_grad = retain * (
        (scaled_back - own_inv * own_inv * wide_gram[own] * along) * own_inv + head_part
    )
    return (latents[None], logits, latent_grad[None])


def solution(mesh):
    return jax.shard_map(
        per_device,
        mesh=mesh,
        in_specs=(
            P("group", "seq", "mp"),
            P(None, "seq"),
            P("seq", "group", "mp"),
            P("mp", None),
            P("group"),
            P("group", "seq", None),
            P(None, "mp"),
            P(None, None, "mp"),
            P("seq", "mp"),
            P("mp", "seq"),
            P(None, "mp", None),
            P(),
            P(),
            P("group", None),
        ),
        out_specs=(P("group", "seq", None), P("group", None, "seq"), P("group", "seq", None)),
        check_vma=False,
    )
```

time: 861 us -> 213 us (0.25)
  waiting for transfers between devices: 683 us -> 85.4 us
  blocking collectives: 88.4 us -> 56.2 us
  matrix products: 57.1 us -> 26.3 us
    all_gather x2 -> x0, waiting for transfers between devices: 637 us -> none  [the longest x1 354 us: per_device(): down_full = lax.all_gather(down_weight, 'seq', axis=1, tiled=True)]
    psum x1 -> x4, waiting for transfers between devices: 19.2 us -> 81.8 us  [the longest x1 40.4 us: per_device(): lax.psum(jnp.dot(down_weight, proj_chunk, preferred_element_type=f32).ast...]
    dot_general x11 -> x13, matrix products: 57.1 us -> 26.3 us  [the longest x1 3.25 us: per_device(): lax.dot_general(preact_grad, up_fold, (((1,), (1,)), ((), ())), preferred...]
    psum x1, blocking collectives: 64.6 us -> 38.4 us  [per_device(): half_mod = lax.psum(half_mod, 'seq')]
    reduce_scatter x2 -> x0, waiting for transfers between devices: 15.9 us -> none  [the longest x1 8.32 us: per_device(): lax.psum_scatter(out_terms.astype(jnp.bfloat16), 'mp', scatter_dimension=...]
  transfers between devices with their start and end apart: 9 -> 6, of which waited for: 9 -> 5; matrix products, arithmetic and copies ran while one was open for 2% -> 9% of each run, Pallas kernels for 0% -> 0%
where the time goes in v1:
time: 213 us; the launch traced here: 212 us
  waiting for transfers between devices  85.4 us (40%)
  blocking collectives  56.2 us (26%)
  matrix products  26.3 us (12%)
  between operations  18.7 us (9%)
  other arithmetic  12.6 us (6%)
  local copies, waits for them, and re-layouts  9.95 us (5%)
  starting transfers between devices  2.75 us (1%)
    psum x1, waiting for transfers between devices, per_device(): lax.psum(jnp.dot(down_weight, proj_chunk, preferred_element_type=f32).ast...  40.4 us
    psum x1, blocking collectives, per_device(): half_mod = lax.psum(half_mod, 'seq')  38.4 us
    psum x1, waiting for transfers between devices, per_device(): lax.psum(jnp.einsum('cd,kdh->kch', teacher_embed, head_proj, preferred_el...  20.1 us
    psum x1, waiting for transfers between devices, per_device(): lax.psum(jnp.dot(activated, out_fold, preferred_element_type=f32).astype(...  10.7 us
    psum x1, waiting for transfers between devices, per_device(): proj_chunk = lax.psum(own_proj, 'mp')  10.5 us
    unnamed x58, local copies, waits for them, and re-layouts  4.79 us
    all_gather x1, blocking collectives, per_device(): halves_all = lax.all_gather(half_mod, 'group', axis=1, tiled=True)  4.39 us
  transfers between devices with their start and end apart: 6, of which 5 were waited for; matrix products, arithmetic and copies ran while one was open for 9% of the time, Pallas kernels for 0%

profile of v1, /device:TPU:0, one launch (start us, length us, event | category | flops | bytes accessed | tf_op | source)
XLA Modules:
  0.0 211.9 jit_solution(798969931426063327)
XLA Ops:
  8.2 1.3 convert_convert_fusion.1
  14.0 1.0 constant_dynamic-slice_fusion.1
  16.7 2.1 %fusion.14 = f32[1,2,1536]{2,0,1:T(1,128)S(1)} fusion(bf16[256,2,1536]{2,1,0:T(2,128)(2,1)} %param.21, f32[1,128]{1,0:T(1,128)S(1)} %get-tuple-element.45, f32[1,128]{1,0:T(1,128)S(1)} %get-tuple-element.46), kind=kOutput, calls=%fused_computation.21 | convolution fusion | flops 9437440 | bytes 1586176 | tf_op jit(solution)/shard_map/f,fjd->jd/dot_general | solution.py:96
  18.9 1.9 all_gather.11
  20.9 2.1 all_gather.10
  23.3 3.1 %convolution_convert_fusion.1 = bf16[65,3072]{1,0:T(8,128)(2,1)} fusion(bf16[384,3072]{1,0:T(8,128)(2,1)} %param.22, s32[]{:T(128)S(6)} %select_n.45, bf16[64,3072]{1,0:T(8,128)(2,1)S(1)} %fusion.29, bf16[1,3072]{1,0:T(2,128)(2,1)S(1)} %slice.364), kind=kOutput, calls=%fused_computation.11 | convolution fusion | flops 153653760 | bytes 3158020 | tf_op jit(solution)/shard_map/dot_general | solution.py:127
  26.3 10.5 %all-reduce.13.cloned.1.call-done = bf16[384,256]{0,1:T(8,128)(2,1)} async-done(((bf16[384,256]{0,1:T(8,128)(2,1)}), bf16[384,256]{0,1:T(8,128)(2,1)}) %all-reduce.13.cloned.1.call-update) | async-done | bytes 196624 | tf_op jit(solution)/shard_map/psum | solution.py:115
  36.9 3.1 %fusion.5 = bf16[3072,256]{0,1:T(8,128)(2,1)} fusion(bf16[384,256]{0,1:T(8,128)(2,1)} %all-reduce.13.cloned.1.call-done, bf16[3072,384]{1,0:T(8,128)(2,1)S(1)} %copy-done), kind=kOutput, calls=%fused_computation.9 | convolution fusion | flops 604766208 | bytes 4128768 | tf_op jit(solution)/shard_map/dot_general | solution.py:117
  41.3 2.5 %all-reduce.4 = (f32[128]{0:T(128)S(1)}, f32[128]{0:T(128)S(1)}) all-reduce(f32[128]{0:T(128)S(1)} %fusion.34, f32[128]{0:T(128)S(1)} %convert_reduce_fusion.1), channel_id=1, replica_groups=mesh['group'=2,'seq'=8,'mp'=2] {'mp'}, use_global_device_ids=true, to_apply=%region_3.4 | all-reduce | flops 256 | bytes 2048 | tf_op jit(solution)/shard_map/psum | solution.py:134
  43.7 1.8 convolution_bitcast_fusion
  45.6 38.4 %psum.72 = f32[2,1,1536]{2,0,1:T(2,128)S(1)} all-reduce(f32[2,1,1536]{2,0,1:T(2,128)S(1)} %convolution_bitcast_fusion), channel_id=1, replica_groups=mesh['group'=2,'seq'=8,'mp'=2] {'seq'}, use_global_device_ids=true, to_apply=%region_4.5 | all-reduce | flops 3072 | bytes 24576 | tf_op jit(solution)/shard_map/psum | solution.py:140
  83.9 4.4 %all_gather.9 = f32[2,2,1536]{2,0,1:T(2,128)S(1)} all-gather(f32[2,1,1536]{2,0,1:T(2,128)S(1)} %psum.72), channel_id=1, replica_groups=mesh['group'=2,'seq'=8,'mp'=2] {'group'}, dimensions={1}, use_global_device_ids=true | all-gather | bytes 36864 | tf_op jit(solution)/shard_map/all_gather | solution.py:141
  88.4 1.3 convolution_convert_fusion.2
  89.7 3.4 %psum.73 = bf16[128,64]{0,1:T(8,128)(2,1)S(1)} all-reduce(bf16[128,64]{0,1:T(8,128)(2,1)S(1)} %convolution_convert_fusion.2), channel_id=1, replica_groups=mesh['group'=2,'seq'=8,'mp'=2] {'mp'}, use_global_device_ids=true, to_apply=%region_5.6 | all-reduce | flops 8192 | bytes 32768 | tf_op jit(solution)/shard_map/psum | solution.py:146
  93.7 1.3 collective-permute-start
  95.0 1.3 collective-permute-start.1
  96.3 0.9 fusion.28
  97.2 3.5 %collective-permute-done.1 = bf16[128,64]{0,1:T(8,128)(2,1)S(1)} collective-permute-done((bf16[128,64]{0,1:T(8,128)(2,1)S(1)}, bf16[128,64]{0,1:T(8,128)(2,1)S(1)}, u32[]{:S(2)}, u32[]{:S(2)}) %collective-permute-start.1) | collective-permute-done | bytes 16416 | tf_op jit(solution)/shard_map/ppermute | solution.py:157
  101.7 40.4 %all-reduce.17.cloned.1.call-done = (bf16[3072,256]{0,1:T(8,128)(2,1)}, bf16[65,3072]{1,0:T(8,128)(2,1)}) async-done(((bf16[3072,256]{0,1:T(8,128)(2,1)}, bf16[65,3072]{1,0:T(8,128)(2,1)}), (bf16[3072,256]{0,1:T(8,128)(2,1)}, bf16[65,3072]{1,0:T(8,128)(2,1)})) %all-reduce.17.cloned.1.call-update) | async-done | bytes 1972240 | tf_op jit(solution)/shard_map/psum | solution.py:116
  142.9 1.9 multiply_add_fusion.1
  144.9 2.1 copy-done.1
  147.0 2.3 %fusion.19 = bf16[384,256]{1,0:T(8,128)(2,1)} fusion(bf16[3072,256]{0,1:T(8,128)(2,1)S(1)} %copy-done.28, f32[384,3072]{1,0:T(8,128)S(1)} %multiply_add_fusion.1), kind=kOutput, calls=%fused_computation.27 | convolution fusion | flops 614694912 | bytes 6488064 | tf_op jit(solution)/shard_map/dot_general | solution.py:169
  149.4 2.4 %convolution_bitcast_fusion.2 = f32[4,64,128]{2,1,0:T(8,128)} fusion(bf16[4,1536,128]{2,1,0:T(8,128)(2,1)} %param.24, bf16[64,1536]{1,0:T(8,128)(2,1)S(1)} %copy-done.3), kind=kOutput, calls=%fused_computation.28 | convolution fusion | flops 100663296 | bytes 1900544 | tf_op jit(solution)/shard_map/cd,kdh->kch/dot_general | solution.py:130
  156.7 10.7 %all-reduce.15.cloned.1.call-done = bf16[384,256]{1,0:T(8,128)(2,1)} async-done(((bf16[384,256]{1,0:T(8,128)(2,1)}), bf16[384,256]{1,0:T(8,128)(2,1)}) %all-reduce.15.cloned.1.call-update) | async-done | bytes 196624 | tf_op jit(solution)/shard_map/psum | solution.py:168
  167.3 1.0 fusion.121
  168.5 20.1 %all-reduce.11.cloned.1.call-done = f32[4,64,128]{2,1,0:T(8,128)} async-done(((f32[4,64,128]{2,1,0:T(8,128)}), f32[4,64,128]{2,1,0:T(8,128)}) %all-reduce.11.cloned.1.call-update) | async-done | bytes 131088 | tf_op jit(solution)/shard_map/psum | solution.py:129
  188.7 1.5 fusion.16
  190.2 1.2 copy.34
  191.3 1.3 broadcast_multiply_fusion
  195.1 3.2 %fusion.17 = f32[128,64]{0,1:T(8,128)S(1)} fusion(bf16[3072,256]{0,1:T(8,128)(2,1)} %get-tuple-element.9, f32[384,3072]{1,0:T(8,128)} %copy-done.1, bf16[65,3072]{1,0:T(8,128)(2,1)} %get-tuple-element.10, bf16[128,128]{1,0:T(8,128)(2,1)S(1)} %bitcast.119, bf16[128,128]{1,0:T(8,128)(2,1)S(1)} %bitcast.118), kind=kOutput, calls=%fused_computation.25 | convolution fusion | flops 259260416 | bytes 3637248 | tf_op jit(solution)/shard_map/dot_general | solution.py:203
  198.4 3.6 %psum.79 = f32[128,64]{0,1:T(8,128)S(1)} all-reduce(f32[128,64]{0,1:T(8,128)S(1)} %fusion.17), channel_id=1, replica_groups=mesh['group'=2,'seq'=8,'mp'=2] {'mp'}, use_global_device_ids=true, to_apply=%region_19.20 | all-reduce | flops 8192 | bytes 65536 | tf_op jit(solution)/shard_map/psum | solution.py:202
  203.7 1.6 fusion.24
  (107 shorter events, 15.9 us)
Async XLA Ops:
  7.2 29.7 %copy-start = (bf16[3072,384]{1,0:T(8,128)(2,1)S(1)}, bf16[3072,384]{1,0:T(8,128)(2,1)}, u32[]{:S(2)}) copy-start(bf16[3072,384]{1,0:T(8,128)(2,1)} %param.23) | copy-start | bytes 7077892
  7.2 29.7 %all-reduce.13.cloned.1.call-start = ((), (), s32[]{:S(2)}) async-start(), calls=%async_computation.1 | async-start | bytes 393216 | tf_op jit(solution)/shard_map/psum | solution.py:115
  7.3 13.6 %copy-start.3 = (bf16[64,1536]{1,0:T(8,128)(2,1)S(1)}, bf16[64,1536]{1,0:T(8,128)(2,1)}, u32[]{:S(2)}) copy-start(bf16[64,1536]{1,0:T(8,128)(2,1)} %param.20) | copy-start | bytes 589828
  16.0 126.2 %all-reduce.17.cloned.1.call-start = ((), (), s32[]{:S(2)}) async-start(), calls=%async_computation.3 | async-start | bytes 4030464 | tf_op jit(solution)/shard_map/psum | solution.py:116
  40.0 1.0 copy-start.2
  40.0 3.8 %copy-start.22 = (f32[2,384]{1,0:T(2,128)S(1)}, f32[2,384]{1,0:T(2,128)}, u32[]{:S(2)}) copy-start(f32[2,384]{1,0:T(2,128)} %param.15) | copy-start | bytes 9220
  40.0 127.3 %all-reduce.15.cloned.1.call-start = ((), (), s32[]{:S(2)}) async-start(), calls=%async_computation.2 | async-start | bytes 393216 | tf_op jit(solution)/shard_map/psum | solution.py:168
  41.1 52.5 %copy-start.18 = (bf16[1,128,64]{1,2,0:T(8,128)(2,1)S(1)}, bf16[1,128,64]{1,2,0:T(8,128)(2,1)}, u32[]{:S(2)}) copy-start(bf16[1,128,64]{1,2,0:T(8,128)(2,1)} %param.19) | copy-start | bytes 49156
  93.7 3.5 %collective-permute-start = (bf16[128,64]{0,1:T(8,128)(2,1)S(1)}, bf16[128,64]{0,1:T(8,128)(2,1)S(1)}, u32[]{:S(2)}, u32[]{:S(2)}) collective-permute-start(bf16[128,64]{0,1:T(8,128)(2,1)S(1)} %fusion.93), channel_id=1, source_target_pairs={{0,2},{2,4},{4,6},{6,8},{8,10},{10,12},{12,14},{1,3},{3,5},{5,7},{... | collective-permute-start | bytes 49160 | tf_op jit(solution)/shard_map/ppermute | solution.py:156
  95.0 5.8 %collective-permute-start.1 = (bf16[128,64]{0,1:T(8,128)(2,1)S(1)}, bf16[128,64]{0,1:T(8,128)(2,1)S(1)}, u32[]{:S(2)}, u32[]{:S(2)}) collective-permute-start(bf16[128,64]{0,1:T(8,128)(2,1)S(1)} %fusion.93), channel_id=1, source_target_pairs={{2,0},{4,2},{6,4},{8,6},{10,8},{12,10},{14,12},{3,1},{5,3},{7,5},{... | collective-permute-start | bytes 49160 | tf_op jit(solution)/shard_map/ppermute | solution.py:157
  97.2 58.8 %copy-start.5 = (bf16[128,64]{0,1:T(8,128)(2,1)}, bf16[128,64]{0,1:T(8,128)(2,1)S(1)}, u32[]{:S(2)}) copy-start(bf16[128,64]{0,1:T(8,128)(2,1)S(1)} %collective-permute-done) | copy-start | bytes 49156
  100.8 55.2 %copy-start.6 = (bf16[128,64]{0,1:T(8,128)(2,1)}, bf16[128,64]{0,1:T(8,128)(2,1)S(1)}, u32[]{:S(2)}) copy-start(bf16[128,64]{0,1:T(8,128)(2,1)S(1)} %collective-permute-done.1) | copy-start | bytes 49156
  142.9 4.1 %copy-start.28 = (bf16[3072,256]{0,1:T(8,128)(2,1)S(1)}, bf16[3072,256]{0,1:T(8,128)(2,1)}, u32[]{:S(2)}) copy-start(bf16[3072,256]{0,1:T(8,128)(2,1)} %get-tuple-element.9) | copy-start | bytes 4718596
  144.9 2.1 %copy-start.1 = (f32[384,3072]{1,0:T(8,128)}, f32[384,3072]{1,0:T(8,128)S(1)}, u32[]{:S(2)}) copy-start(f32[384,3072]{1,0:T(8,128)S(1)} %multiply_add_fusion.1) | copy-start | bytes 14155780
  149.3 4.2 %copy-start.17 = (f32[4,3,3,128]{3,0,2,1:T(4,128)S(1)}, f32[4,3,3,128]{3,0,2,1:T(4,128)}, u32[]{:S(2)}) copy-start(f32[4,3,3,128]{3,0,2,1:T(4,128)} %param.25) | copy-start | bytes 55300
  149.3 5.5 %copy-start.20 = (f32[4,128]{1,0:T(4,128)S(1)}, f32[4,128]{1,0:T(4,128)}, u32[]{:S(2)}) copy-start(f32[4,128]{1,0:T(4,128)} %param.26) | copy-start | bytes 6148
  149.3 39.3 %all-reduce.11.cloned.1.call-start = ((), (), s32[]{:S(2)}) async-start(), calls=%async_computation | async-start | bytes 262144 | tf_op jit(solution)/shard_map/psum | solution.py:129
  192.7 0.7 copy-start.8
  192.7 0.7 copy-start.9
  192.7 0.7 copy-start.11
  192.7 0.7 copy-start.12
  192.7 0.7 copy-start.13
  192.7 0.7 copy-start.14
  192.7 0.7 copy-start.15
  192.7 0.7 copy-start.16
  192.7 0.7 copy-start.19
  192.8 0.7 copy-start.27
  194.1 0.7 copy-start.24
  195.1 7.8 %copy-start.21 = (f32[4,128]{1,0:T(4,128)S(1)}, f32[4,128]{1,0:T(4,128)}, u32[]{:S(2)}) copy-start(f32[4,128]{1,0:T(4,128)} %param.26) | copy-start | bytes 6148
  198.4 5.4 %copy-start.4 = (f32[4,64,128]{2,1,0:T(8,128)S(1)}, f32[4,64,128]{2,1,0:T(8,128)}, u32[]{:S(2)}) copy-start(f32[4,64,128]{2,1,0:T(8,128)} %all-reduce.11.cloned.1.call-done) | copy-start | bytes 393220
  198.4 5.4 %copy-start.25 = (f32[128]{0:T(128)S(1)}, f32[128]{0:T(128)}, u32[]{:S(2)}) copy-start(f32[128]{0:T(128)} %get-tuple-element.35) | copy-start | bytes 1540
  198.4 5.4 %copy-start.26 = (f32[128]{0:T(128)S(1)}, f32[128]{0:T(128)}, u32[]{:S(2)}) copy-start(f32[128]{0:T(128)} %get-tuple-element.36) | copy-start | bytes 1540
  (3 other events, 1.8 us)
Sparse Core Ops, SparseCore 0:
  16.1 20.7 all-reduce.12
  40.5 101.5 all-reduce.16
  149.5 17.7 all-reduce.14
  169.6 19.0 all-reduce.10

commit v2 on v1

--- a/solution.py
+++ b/solution.py
@@ -1,8 +1,11 @@
+import functools
 import math
 
 import jax
 import jax.numpy as jnp
 from jax import lax
+from jax.experimental import pallas as pl
+from jax.experimental.pallas import tpu as pltpu
 from jax.sharding import PartitionSpec as P
 
 GRID_W = 64
@@ -31,6 +34,165 @@
     freqs = jnp.exp(-math.log(10000.0) * index / half_width)
     angles = timestep.astype(jnp.float32)[:, None] * freqs[None, :]
     return jnp.concatenate([jnp.cos(angles), jnp.sin(angles)], axis=-1)
+
+
+MESH = pl.DeviceIdType.MESH
+NEAR = 2
+PIECES = 4
+
+
+def fold_kernel(
+    n_group, n_seq, pieces, fold_ref, mod_ref, out_ref, mod_out_ref,
+    near_in, part, far_in, mod_in, near_sems, far_sems, back_sems, last_sems, mod_sems,
+):
+    far = n_seq // NEAR
+    group, seq = lax.axis_index("group"), lax.axis_index("seq")
+    my_far, my_near = seq // NEAR, lax.rem(seq, NEAR)
+    other = lax.rem(my_near + 1, NEAR)
+    piece = fold_ref.shape[2] // pieces
+    f32 = jnp.float32
+
+    partners = [(dg, ds) for dg in range(n_group) for ds in range(n_seq) if dg or ds]
+    barrier = pltpu.get_barrier_semaphore()
+    for dg, ds in partners:
+        target = {"group": lax.rem(group + dg, n_group), "seq": lax.rem(seq + ds, n_seq)}
+        pl.semaphore_signal(barrier, inc=1, device_id=target, device_id_type=MESH)
+    pl.semaphore_wait(barrier, len(partners))
+
+    def far_id(step):
+        return lax.rem(my_far + step, far) * NEAR + my_near
+
+    def rows(s):
+        return pl.ds(s * piece, piece)
+
+    mod_copies = []
+    for dg, ds in partners:
+        to_group = lax.rem(group + dg, n_group)
+        copy = pltpu.make_async_remote_copy(
+            src_ref=mod_ref.at[to_group],
+            dst_ref=mod_in.at[dg, ds],
+            send_sem=mod_sems.at[0, dg, ds],
+            recv_sem=mod_sems.at[1, dg, ds],
+            device_id={"group": to_group, "seq": lax.rem(seq + ds, n_seq)},
+            device_id_type=MESH,
+        )
+        copy.start()
+        mod_copies.append(copy)
+    near_copies = []
+    for s in range(pieces):
+        copy = pltpu.make_async_remote_copy(
+            src_ref=fold_ref.at[other, :, rows(s)],
+            dst_ref=near_in.at[:, rows(s)],
+            send_sem=near_sems.at[0, s],
+            recv_sem=near_sems.at[1, s],
+            device_id={"seq": my_far * NEAR + other},
+            device_id_type=MESH,
+        )
+        copy.start()
+        near_copies.append(copy)
+    mod_in[0, 0] = mod_ref[group]
+
+    far_copies, back_copies, last_copies = {}, {}, {}
+    for s in range(pieces):
+        near_copies[s].wait_recv()
+        part[:, rows(s)] = (
+            fold_ref[my_near, :, rows(s)].astype(f32) + near_in[:, rows(s)].astype(f32)
+        ).astype(part.dtype)
+        for k in range(1, far):
+            copy = pltpu.make_async_remote_copy(
+                src_ref=part.at[lax.rem(my_far + k, far), rows(s)],
+                dst_ref=far_in.at[k - 1, rows(s)],
+                send_sem=far_sems.at[0, s, k - 1],
+                recv_sem=far_sems.at[1, s, k - 1],
+                device_id={"seq": far_id(k)},
+                device_id_type=MESH,
+            )
+            copy.start()
+            far_copies[s, k] = copy
+
+    def finish(s):
+        for k in range(1, far):
+            back_copies[s, k].wait_recv()
+        copy = pltpu.make_async_remote_copy(
+            src_ref=out_ref.at[my_near, :, rows(s)],
+            dst_ref=out_ref.at[my_near, :, rows(s)],
+            send_sem=last_sems.at[0, s],
+            recv_sem=last_sems.at[1, s],
+            device_id={"seq": my_far * NEAR + other},
+            device_id_type=MESH,
+        )
+        copy.start()
+        last_copies[s] = copy
+
+    for s in range(pieces):
+        total = part[my_far, rows(s)].astype(f32)
+        for k in range(1, far):
+            far_copies[s, k].wait_recv()
+            total = total + far_in[k - 1, rows(s)].astype(f32)
+        out_ref[my_near, my_far, rows(s)] = total.astype(out_ref.dtype)
+        for k in range(1, far):
+            copy = pltpu.make_async_remote_copy(
+                src_ref=out_ref.at[my_near, my_far, rows(s)],
+                dst_ref=out_ref.at[my_near, my_far, rows(s)],
+                send_sem=back_sems.at[0, s, k - 1],
+                recv_sem=back_sems.at[1, s, k - 1],
+                device_id={"seq": far_id(k)},
+                device_id_type=MESH,
+            )
+            copy.start()
+            back_copies[s, k] = copy
+        if s >= 1:
+            finish(s - 1)
+    for copy in mod_copies:
+        copy.wait_recv()
+    for dg in range(n_group):
+        total = mod_in[dg, 0]
+        for ds in range(1, n_seq):
+            total = total + mod_in[dg, ds]
+        mod_out_ref[lax.rem(group + n_group - dg, n_group)] = total
+    finish(pieces - 1)
+    for s in range(pieces):
+        last_copies[s].wait_recv()
+    for copies in (mod_copies, near_copies, far_copies.values(), back_copies.values(), last_copies.values()):
+        for copy in copies:
+            copy.wait_send()
+
+
+def summed_folds(fold, mod, n_group, n_seq):
+    hidden, lanes = fold.shape
+    share = hidden // n_seq
+    far = n_seq // NEAR
+    mod_rows = mod.shape[1] // 128
+    fits = hidden % n_seq == 0 and n_seq % NEAR == 0 and far > 1 and share % (16 * PIECES) == 0
+    if not fits or mod.shape[1] % 128 or mod.shape[0] != n_group:
+        halves = lax.all_gather(lax.psum(mod, "seq"), "group", axis=1)
+        own = lax.dynamic_slice_in_dim(halves, lax.axis_index("group"), 1, 0)[0]
+        return lax.psum(fold, "seq"), own
+    dma = pltpu.SemaphoreType.DMA
+    summed, own = pl.pallas_call(
+        functools.partial(fold_kernel, n_group, n_seq, PIECES),
+        out_shape=(
+            jax.ShapeDtypeStruct((NEAR, far, share, lanes), fold.dtype),
+            jax.ShapeDtypeStruct((n_group, mod_rows, 128), jnp.float32),
+        ),
+        in_specs=[pl.BlockSpec(memory_space=pltpu.VMEM)] * 2,
+        out_specs=(pl.BlockSpec(memory_space=pltpu.VMEM),) * 2,
+        scratch_shapes=[
+            pltpu.VMEM((far, share, lanes), fold.dtype),
+            pltpu.VMEM((far, share, lanes), fold.dtype),
+            pltpu.VMEM((far - 1, share, lanes), fold.dtype),
+            pltpu.VMEM((n_group, n_seq, mod_rows, 128), jnp.float32),
+            dma((2, PIECES)),
+            dma((2, PIECES, far - 1)),
+            dma((2, PIECES, far - 1)),
+            dma((2, PIECES)),
+            dma((2, n_group, n_seq)),
+        ],
+        compiler_params=pltpu.CompilerParams(
+            collective_id=0, has_side_effects=True, vmem_limit_bytes=40 * 1024 * 1024
+        ),
+    )(fold.reshape(NEAR, far, share, lanes), mod.reshape(mod.shape[0], mod_rows, 128))
+    return summed.reshape(hidden, lanes), own.reshape(n_group, mod.shape[1])
 
 
 def shifted(grid, offset):
@@ -111,11 +273,9 @@
         ],
         axis=1,
     ).reshape(chunk, picked * channels)
-    own_proj = jnp.where(lax.axis_index("mp") == owner, own_proj, jnp.zeros_like(own_proj))
-    proj_chunk = lax.psum(own_proj, "mp")
-    out_fold = lax.psum(
-        jnp.dot(down_weight, proj_chunk, preferred_element_type=f32).astype(bf16), "seq"
-    )
+    own_proj = lax.all_gather(own_proj, "mp")
+    proj_chunk = lax.dynamic_index_in_dim(own_proj, owner, 0, keepdims=False)
+    out_terms = jnp.dot(down_weight, proj_chunk, preferred_element_type=f32).astype(bf16)
     embed_f = embed_full.astype(f32)
     embed_centered = embed_f - jnp.mean(embed_f, axis=1, keepdims=True)
     gram = jnp.einsum("cd,ed->ce", embed_centered, embed_centered, precision=highest)
@@ -123,12 +283,13 @@
         [embed_centered * (1.0 + tmod[1:2]), tmod[0:1]], axis=0
     ).astype(bf16)
     stacked = lax.dynamic_slice_in_dim(stacked, start, chunk, 1)
-    in_fold = lax.psum(
-        jnp.dot(stacked, up_weight, preferred_element_type=f32).astype(bf16), "seq"
-    )
-    embed_proj = lax.psum(
-        jnp.einsum("cd,kdh->kch", teacher_embed, head_proj, preferred_element_type=f32), "mp"
-    )
+    pad = -stacked.shape[0] % 128
+    stacked = jnp.pad(stacked, ((0, pad), (0, 0)))
+    in_terms = lax.dot_general(
+        up_weight, stacked, (((0,), (1,)), ((), ())), preferred_element_type=f32
+    ).astype(bf16)
+    embed_proj = jnp.einsum("cd,kdh->kch", teacher_embed, head_proj, preferred_element_type=f32)
+    embed_proj = jnp.sum(lax.all_gather(embed_proj, "mp"), axis=0)
 
     hidden = student_hidden[0].astype(f32)
     first_sum, square_sum = lax.psum((jnp.sum(hidden, -1), jnp.sum(hidden * hidden, -1)), "mp")
@@ -137,9 +298,15 @@
     half_mod = jnp.einsum(
         "sk,kjd->sjd", student_cond, student_mod.astype(f32), precision=highest
     )
-    half_mod = lax.psum(half_mod, "seq")
-    halves_all = lax.all_gather(half_mod, "group", axis=1, tiled=True)
-    own_mod = lax.dynamic_slice_in_dim(halves_all, lax.axis_index("group"), 1, 0)[0]
+    folds, own_mod = summed_folds(
+        jnp.concatenate([out_terms, in_terms], axis=1),
+        half_mod[:, 0],
+        lax.axis_size("group"),
+        n_seq,
+    )
+    out_fold = folds[:, : picked * channels]
+    up_fold = folds[:, picked * channels : picked * channels + latent_width]
+    bias = folds[:, picked * channels + latent_width].astype(f32)[None]
     normed = (
         (hidden - tok_mean) * lax.rsqrt(tok_var + EPSILON) * (1.0 + own_mod[1:2]) + own_mod[0:1]
     ).astype(bf16)
@@ -161,13 +328,14 @@
     wide_gram = jnp.dot(wide_f, gram, precision=highest)
     var_t = jnp.sum(wide_f * wide_gram, -1, keepdims=True) / width
     inv_std = lax.rsqrt(var_t + EPSILON)
-    up_fold = in_fold[:latent_width]
-    bias = in_fold[latent_width:].astype(f32)
-    preact = inv_std * jnp.dot(wide, up_fold, preferred_element_type=f32) + bias
+    preact = (
+        inv_std
+        * lax.dot_general(wide, up_fold, (((1,), (1,)), ((), ())), preferred_element_type=f32)
+        + bias
+    )
     activated = gelu_tanh(preact).astype(bf16)
-    block_terms = lax.psum(
-        jnp.dot(activated, out_fold, preferred_element_type=f32).astype(bf16), "mp"
-    ).astype(f32)
+    block_terms = jnp.dot(activated, out_fold, preferred_element_type=f32).astype(bf16)
+    block_terms = jnp.sum(lax.all_gather(block_terms, "mp").astype(f32), axis=0)
     projected = jnp.einsum("tc,kch->kth", wide_f, embed_proj, precision=highest)
     projected = projected + sum(
         one_hot[:, j][:, None, None]
@@ -200,9 +368,7 @@
     own = slice(halo, halo + tokens)
     preact_grad = (hidden_grad * gelu_slope(preact[own])).astype(bf16)
     scaled_back = lax.psum(
-        lax.dot_general(
-            preact_grad, up_fold, (((1,), (1,)), ((), ())), preferred_element_type=f32
-        ),
+        jnp.dot(preact_grad, up_fold, preferred_element_type=f32),
         "mp",
     )
     noised_f, own_inv = wide_f[own], inv_std[own]

time: 213 us -> 166 us (0.78)
  waiting for transfers between devices: 85.4 us -> 0.01 us
  Pallas kernels: 0 us -> 78.2 us
  blocking collectives: 56.2 us -> 19.8 us
  between operations: 18.7 us -> 6.01 us
  local copies, waits for them, and re-layouts: 9.95 us -> 16.6 us
  matrix products: 26.3 us -> 22.6 us
  starting transfers between devices: 2.75 us -> 5.84 us
    psum x4 -> x0, waiting for transfers between devices: 81.8 us -> none  [the longest x1 40.4 us: per_device(): lax.psum(jnp.dot(down_weight, proj_chunk, preferred_element_type=f32).ast...]
    pallas_call x0 -> x1, Pallas kernels: none -> 78.2 us  [summed_folds(): pl.pallas_call(functools.partial(fold_kernel, n_group, n_seq, PIECES), ou...]
    psum x2 -> x1, blocking collectives: 41.9 us -> 3.41 us  [per_device(): lax.psum(jnp.dot(preact_grad, up_fold, preferred_element_type=f32), 'mp')]
    concatenate x0 -> x1, local copies, waits for them, and re-layouts: none -> 4.27 us  [per_device(): jnp.concatenate([out_terms, in_terms], axis=1)]
    ppermute x1, waiting for transfers between devices: 3.55 us -> 0.01 us  [per_device(): after = lax.ppermute(noised[:halo], 'seq', downs)]
    ppermute x1, starting transfers between devices: 1.29 us -> 4.55 us  [per_device(): before = lax.ppermute(noised[tokens - halo:], 'seq', ups)]
    convert_element_type x0 -> x1, other arithmetic: none -> 2.57 us  [per_device(): bias = folds[:, picked * channels + latent_width].astype(f32)[None]]
    unnamed x58 -> x68, local copies, waits for them, and re-layouts: 4.79 us -> 7.35 us
  transfers between devices with their start and end apart: 6 -> 2, of which waited for: 5 -> 0; matrix products, arithmetic and copies ran while one was open for 9% -> 6% of each run, Pallas kernels for 0% -> 0%
where the time goes in v2:
time: 166 us; the launch traced here: 164 us
  Pallas kernels  78.2 us (47%)
  matrix products  22.6 us (14%)
  blocking collectives  19.8 us (12%)
  local copies, waits for them, and re-layouts  16.6 us (10%)
  other arithmetic  14.6 us (9%)
  between operations  6.01 us (4%)
  starting transfers between devices  5.84 us (4%)
    pallas_call x1, Pallas kernels, summed_folds(): pl.pallas_call(functools.partial(fold_kernel, n_group, n_seq, PIECES), ou...  78.2 us
    unnamed x68, local copies, waits for them, and re-layouts  7.35 us
    ppermute x1, starting transfers between devices, per_device(): before = lax.ppermute(noised[tokens - halo:], 'seq', ups)  4.55 us
    concatenate x1, local copies, waits for them, and re-layouts, per_device(): jnp.concatenate([out_terms, in_terms], axis=1)  4.27 us
    dot_general x1, matrix products, per_device(): jnp.dot(preact_grad, up_fold, preferred_element_type=f32)  3.52 us
    psum x1, blocking collectives, per_device(): lax.psum(jnp.dot(preact_grad, up_fold, preferred_element_type=f32), 'mp')  3.41 us
    psum x1, blocking collectives, per_device(): lax.psum(jnp.dot(normed, student_out, preferred_element_type=f32).astype(...  3.36 us
  transfers between devices with their start and end apart: 2, of which 0 were waited for; matrix products, arithmetic and copies ran while one was open for 6% of the time, Pallas kernels for 0%

profile of v2, /device:TPU:0, one launch (start us, length us, event | category | flops | bytes accessed | tf_op | source)
XLA Modules:
  0.0 163.8 jit_solution(9047961173679545186)
XLA Ops:
  1.5 2.2 %fusion.15 = f32[1,2,1536]{2,0,1:T(1,128)S(1)} fusion(bf16[256,2,1536]{2,1,0:T(2,128)(2,1)} %param.21, f32[1,128]{1,0:T(1,128)S(1)} %get-tuple-element.47, f32[1,128]{1,0:T(1,128)S(1)} %get-tuple-element.48), kind=kOutput, calls=%fused_computation.22 | convolution fusion | flops 9437440 | bytes 1586176 | tf_op jit(solution)/shard_map/f,fjd->jd/dot_general | solution.py:258
  3.7 1.9 %all_gather.23 = f32[2,3072]{1,0:T(2,128)S(1)} all-gather(f32[2,1536]{1,0:T(2,128)S(1)} %bitcast.137), channel_id=1, replica_groups=mesh['group'=2,'seq'=8,'mp'=2] {'mp'}, dimensions={1}, use_global_device_ids=true | all-gather | bytes 36864 | tf_op jit(solution)/shard_map/all_gather | solution.py:264
  6.5 1.2 convert_convert_fusion.1
  11.0 1.7 %fusion.40 = f32[128]{0:T(128)} fusion(bf16[1,128,1536]{2,1,0:T(8,128)(2,1)} %param.14), kind=kLoop, calls=%fused_computation.49 | loop fusion | flops 589696 | bytes 393728 | tf_op jit(solution)/shard_map/reduce_sum | solution.py:295
  13.3 2.1 %all_gather.22 = bf16[64,3072]{1,0:T(8,128)(2,1)S(1)} all-gather(bf16[64,1536]{1,0:T(8,128)(2,1)S(1)} %copy-done.9), channel_id=1, replica_groups=mesh['group'=2,'seq'=8,'mp'=2] {'mp'}, dimensions={1}, use_global_device_ids=true | all-gather | bytes 589824 | tf_op jit(solution)/shard_map/all_gather | solution.py:257
  18.3 2.2 %all_gather.21 = bf16[2,384,256]{2,1,0:T(8,128)(2,1)} all-gather(bf16[1,384,256]{2,1,0:T(8,128)(2,1)S(1)} %copy.40), channel_id=1, replica_groups=mesh['group'=2,'seq'=8,'mp'=2] {'mp'}, dimensions={0}, use_global_device_ids=true | all-gather | bytes 589824 | tf_op jit(solution)/shard_map/all_gather | solution.py:276
  20.7 2.2 %fusion.7 = bf16[3072,128]{0,1:T(8,128)(2,1)S(1)} fusion(bf16[384,3072]{1,0:T(8,128)(2,1)} %param.22, bf16[65,384]{1,0:T(8,128)(2,1)S(1)} %fusion.95), kind=kOutput, calls=%fused_computation.12 | convolution fusion | flops 302383104 | bytes 3195648 | tf_op jit(solution)/shard_map/dot_general | solution.py:288
  23.0 1.9 %fusion.5 = bf16[3072,256]{0,1:T(8,128)(2,1)S(1)} fusion(bf16[3072,384]{1,0:T(8,128)(2,1)S(1)} %copy-done, bf16[2,384,256]{2,1,0:T(8,128)(2,1)} %all_gather.21, s32[]{:T(128)S(6)} %select_n.40), kind=kOutput, calls=%fused_computation.9 | convolution fusion | flops 604766208 | bytes 4128772 | tf_op jit(solution)/shard_map/dot_general | solution.py:278
  25.0 1.6 pad_maximum_fusion
  26.5 4.3 %copy.41 = bf16[3072,384]{1,0:T(8,128)(2,1)} copy(bf16[3072,384]{0,1:T(8,128)(2,1)} %pad_maximum_fusion) | data formatting | bytes 4718592 | tf_op jit(solution)/shard_map/concatenate | solution.py:302
  30.8 1.7 %copy.42 = bf16[384,1,1536]{0,2,1:T(8,128)(2,1)S(1)} copy(bf16[384,1,1536]{2,0,1:T(8,128)(2,1)} %param.16) | data formatting | bytes 2359296 | tf_op args[2]
  32.5 1.7 %fusion.102 = f32[2,12,128]{2,0,1:T(2,128)S(1)} fusion(bf16[12,128,384]{2,1,0:T(8,128)(2,1)S(1)} %bitcast.128, f32[2,384]{1,0:T(2,128)} %param.15), kind=kOutput, calls=%fused_computation.146 | convolution fusion | flops 14155776 | bytes 1195008 | tf_op jit(solution)/shard_map/sk,kjd->sjd/dot_general | solution.py:298
  34.2 1.7 %copy-done.1 = bf16[3072,384]{1,0:T(8,128)(2,1)S(1)} copy-done((bf16[3072,384]{1,0:T(8,128)(2,1)S(1)}, bf16[3072,384]{1,0:T(8,128)(2,1)}, u32[]{:S(2)}) %copy-start.1) | copy-done | bytes 2359320
  35.9 78.2 %shard_map.157 = (bf16[2,4,384,384]{3,2,1,0:T(8,128)(2,1)S(1)}, f32[2,12,128]{2,1,0:T(8,128)S(1)}) custom-call(bf16[2,4,384,384]{3,2,1,0:T(8,128)(2,1)S(1)} %bitcast.123, f32[2,12,128]{2,1,0:T(8,128)S(1)} %copy.43.mod_ref), custom_call_target="tpu_custom_call" | custom-call | tf_op jit(solution)/shard_map/pallas_call | solution.py:172
  114.2 1.4 copy-done.2
  115.6 2.6 %all-reduce.5 = (f32[128]{0:T(128)S(1)}, f32[128]{0:T(128)S(1)}) all-reduce(f32[128]{0:T(128)} %fusion.40, f32[128]{0:T(128)} %convert_reduce_fusion.1), channel_id=1, replica_groups=mesh['group'=2,'seq'=8,'mp'=2] {'mp'}, use_global_device_ids=true, to_apply=%region_3.4 | all-reduce | flops 256 | bytes 2048 | tf_op jit(solution)/shard_map/psum | solution.py:295
  118.6 3.4 %psum.30 = bf16[128,64]{0,1:T(8,128)(2,1)S(1)} all-reduce(bf16[128,64]{0,1:T(8,128)(2,1)S(1)} %convolution_convert_fusion.2), channel_id=1, replica_groups=mesh['group'=2,'seq'=8,'mp'=2] {'mp'}, use_global_device_ids=true, to_apply=%region_8.9 | all-reduce | flops 8192 | bytes 32768 | tf_op jit(solution)/shard_map/psum | solution.py:313
  122.0 1.3 collective-permute-start.1
  123.3 4.5 %collective-permute-start = (bf16[128,64]{0,1:T(8,128)(2,1)S(1)}, bf16[128,64]{0,1:T(8,128)(2,1)S(1)}, u32[]{:S(2)}, u32[]{:S(2)}) collective-permute-start(bf16[128,64]{0,1:T(8,128)(2,1)S(1)} %fusion.101), channel_id=1, source_target_pairs={{0,2},{2,4},{4,6},{6,8},{8,10},{10,12},{12,14},{1,3},{3,5},{5,7},{... | collective-permute-start | bytes 49160 | tf_op jit(solution)/shard_map/ppermute | solution.py:323
  127.9 1.9 %convolution_bitcast_fusion.1 = f32[4,64,128]{2,1,0:T(8,128)S(1)} fusion(bf16[4,1536,128]{2,1,0:T(8,128)(2,1)} %param.24, bf16[64,1536]{1,0:T(8,128)(2,1)} %param.20), kind=kOutput, calls=%fused_computation.30 | convolution fusion | flops 100663296 | bytes 1900544 | tf_op jit(solution)/shard_map/cd,kdh->kch/dot_general | solution.py:291
  132.5 2.6 %slice_convert_fusion = f32[3072,1]{1,0:T(8,128)} fusion(bf16[3072,384]{1,0:T(8,128)(2,1)} %bitcast.124), kind=kLoop, calls=%fused_computation.50 | loop fusion | flops 3072 | bytes 18432 | tf_op jit(solution)/shard_map/convert_element_type | solution.py:309
  135.1 2.0 %all-gather = f32[8,64,128]{2,1,0:T(8,128)S(1)} all-gather(f32[4,64,128]{2,1,0:T(8,128)S(1)} %convolution_bitcast_fusion.1), channel_id=2, replica_groups=mesh['group'=2,'seq'=8,'mp'=2] {'mp'}, dimensions={0}, use_global_device_ids=true | all-gather | bytes 393216 | tf_op jit(solution)/shard_map/all_gather | solution.py:292
  137.7 1.9 %copy.51 = f32[3072,1]{0,1:T(1,128)S(1)} copy(f32[3072,1]{1,0:T(8,128)} %slice_convert_fusion) | data formatting | bytes 24576
  141.1 2.2 %multiply_add_fusion.1 = f32[384,3072]{1,0:T(8,128)S(1)} fusion(f32[3072]{0:T(1024)S(1)} %bitcast.139, f32[384]{0:T(512)S(1)} %add_rsqrt_fusion, bf16[3072,384]{1,0:T(8,128)(2,1)} %bitcast.125, bf16[128,64]{0,1:T(8,128)(2,1)S(1)} %collective-permute-done.1, bf16[128,64]{0,1:T(8,128)(2,1)S(1)} %fusion.101, bf16[128,64]{0,1:T(8,128)(2,1)S(1)} %collective-permute-done), kind=kOutput, calls=%fused_computation.6 | convolution fusion | flops 153501696 | bytes 5568000 | tf_op jit(solution)/shard_map/dot_general | solution.py:333
  143.3 1.6 fusion.23
  145.4 2.3 %all-gather.1 = bf16[768,256]{1,0:T(8,128)(2,1)S(1)} all-gather(bf16[384,256]{1,0:T(8,128)(2,1)S(1)} %fusion.23), channel_id=3, replica_groups=mesh['group'=2,'seq'=8,'mp'=2] {'mp'}, dimensions={0}, use_global_device_ids=true | all-gather | bytes 589824 | tf_op jit(solution)/shard_map/all_gather | solution.py:338
  148.8 1.5 fusion.19
  150.2 1.1 copy.47
  151.4 1.3 broadcast_multiply_fusion
  155.1 3.5 %fusion.21 = f32[128,64]{0,1:T(8,128)S(1)} fusion(f32[384,3072]{1,0:T(8,128)} %copy-done.4, bf16[3072,384]{1,0:T(8,128)(2,1)} %bitcast.126, bf16[128,128]{1,0:T(8,128)(2,1)S(1)} %bitcast.141, bf16[128,128]{1,0:T(8,128)(2,1)S(1)} %bitcast.140), kind=kOutput, calls=%fused_computation.28 | convolution fusion | flops 259260416 | bytes 4030464 | tf_op jit(solution)/shard_map/dot_general | solution.py:371
  158.6 3.4 %psum.31 = f32[128,64]{0,1:T(8,128)S(1)} all-reduce(f32[128,64]{0,1:T(8,128)S(1)} %fusion.21), channel_id=1, replica_groups=mesh['group'=2,'seq'=8,'mp'=2] {'mp'}, use_global_device_ids=true, to_apply=%region_15.16 | all-reduce | flops 8192 | bytes 65536 | tf_op jit(solution)/shard_map/psum | solution.py:370
  162.1 1.6 %fusion.30 = f32[1,128,64]{1,2,0:T(8,128)} fusion(bf16[4,128,128]{2,1,0:T(8,128)(2,1)S(1)} %bitcast.133, f32[4,64,128]{2,1,0:T(8,128)S(1)} %reduce_sum.133, f32[128,64]{0,1:T(8,128)S(1)} %psum.31, f32[384,64]{0,1:T(8,128)} %get-tuple-element.44, f32[128]{0:T(128)S(1)} %copy-done.28, f32[128]{0:T(128)S(1)} %broadcast_multiply_fusion.2, ...), kind=kOutput, calls=%fused_computation.34 | convolution fusion | flops 50380800 | bytes 361988 | tf_op jit(solution)/shard_map/kth,kch->tc/dot_general | solution.py:357
  (114 shorter events, 13.0 us)
Async XLA Ops:
  0.6 22.4 %copy-start = (bf16[3072,384]{1,0:T(8,128)(2,1)S(1)}, bf16[3072,384]{1,0:T(8,128)(2,1)}, u32[]{:S(2)}) copy-start(bf16[3072,384]{1,0:T(8,128)(2,1)} %param.23) | copy-start | bytes 7077892
  0.6 12.1 %copy-start.7 = (bf16[1,128,1536]{2,1,0:T(8,128)(2,1)S(1)}, bf16[1,128,1536]{2,1,0:T(8,128)(2,1)}, u32[]{:S(2)}) copy-start(bf16[1,128,1536]{2,1,0:T(8,128)(2,1)} %param.14) | copy-start | bytes 1179652
  0.7 12.7 %copy-start.9 = (bf16[64,1536]{1,0:T(8,128)(2,1)S(1)}, bf16[64,1536]{1,0:T(8,128)(2,1)}, u32[]{:S(2)}) copy-start(bf16[64,1536]{1,0:T(8,128)(2,1)} %param.20) | copy-start | bytes 589828
  7.7 10.1 %copy-start.23 = (pred[4]{0:T(512)(128)(4,1)}, pred[4]{0:T(512)(128)(4,1)S(1)}, u32[]{:S(2)}) copy-start(pred[4]{0:T(512)(128)(4,1)S(1)} %get-tuple-element.15) | copy-start | bytes 16
  7.7 10.1 %copy-start.25 = (pred[4]{0:T(512)(128)(4,1)}, pred[4]{0:T(512)(128)(4,1)S(1)}, u32[]{:S(2)}) copy-start(pred[4]{0:T(512)(128)(4,1)S(1)} %get-tuple-element.40) | copy-start | bytes 16
  15.4 7.6 %copy-start.5 = (bf16[64,3072]{1,0:T(8,128)(2,1)}, bf16[64,3072]{1,0:T(8,128)(2,1)S(1)}, u32[]{:S(2)}) copy-start(bf16[64,3072]{1,0:T(8,128)(2,1)S(1)} %all_gather.22) | copy-start | bytes 1179652
  15.6 5.1 %copy-start.30 = (f32[64]{0:T(128)}, f32[64]{0:T(128)S(1)}, u32[]{:S(2)}) copy-start(f32[64]{0:T(128)S(1)} %broadcast_multiply_fusion.1) | copy-start | bytes 772
  32.5 89.4 %copy-start.17 = (bf16[1,128,64]{1,2,0:T(8,128)(2,1)S(1)}, bf16[1,128,64]{1,2,0:T(8,128)(2,1)}, u32[]{:S(2)}) copy-start(bf16[1,128,64]{1,2,0:T(8,128)(2,1)} %param.19) | copy-start | bytes 49156
  34.2 1.7 %copy-start.1 = (bf16[3072,384]{1,0:T(8,128)(2,1)S(1)}, bf16[3072,384]{1,0:T(8,128)(2,1)}, u32[]{:S(2)}) copy-start(bf16[3072,384]{1,0:T(8,128)(2,1)} %copy.41) | copy-start | bytes 7077892
  35.9 82.3 %copy-start.8 = (bf16[1,128,1536]{2,1,0:T(8,128)(2,1)S(1)}, bf16[1,128,1536]{2,1,0:T(8,128)(2,1)}, u32[]{:S(2)}) copy-start(bf16[1,128,1536]{2,1,0:T(8,128)(2,1)} %param.14) | copy-start | bytes 1179652
  35.9 82.3 %copy-start.32 = (bf16[1536,64]{0,1:T(8,128)(2,1)S(1)}, bf16[1536,64]{0,1:T(8,128)(2,1)}, u32[]{:S(2)}) copy-start(bf16[1536,64]{0,1:T(8,128)(2,1)} %param.17) | copy-start | bytes 589828
  35.9 93.9 %copy-start.6 = (bf16[64,3072]{1,0:T(8,128)(2,1)S(1)}, bf16[64,3072]{1,0:T(8,128)(2,1)}, u32[]{:S(2)}) copy-start(bf16[64,3072]{1,0:T(8,128)(2,1)} %copy-done.5) | copy-start | bytes 1179652
  35.9 93.9 %copy-start.31 = (f32[64]{0:T(128)S(1)}, f32[64]{0:T(128)}, u32[]{:S(2)}) copy-start(f32[64]{0:T(128)} %copy-done.30) | copy-start | bytes 772
  114.2 1.4 copy-start.2
  115.6 16.3 %copy-start.16 = (f32[4,3,3,128]{3,0,2,1:T(4,128)S(1)}, f32[4,3,3,128]{3,0,2,1:T(4,128)}, u32[]{:S(2)}) copy-start(f32[4,3,3,128]{3,0,2,1:T(4,128)} %param.25) | copy-start | bytes 55300
  121.9 13.2 %copy-start.10 = (bf16[128,64]{0,1:T(8,128)(2,1)}, bf16[128,64]{0,1:T(8,128)(2,1)S(1)}, u32[]{:S(2)}) copy-start(bf16[128,64]{0,1:T(8,128)(2,1)S(1)} %psum.30) | copy-start | bytes 49156
  122.0 17.6 %collective-permute-start.1 = (bf16[128,64]{0,1:T(8,128)(2,1)S(1)}, bf16[128,64]{0,1:T(8,128)(2,1)S(1)}, u32[]{:S(2)}, u32[]{:S(2)}) collective-permute-start(bf16[128,64]{0,1:T(8,128)(2,1)S(1)} %fusion.101), channel_id=1, source_target_pairs={{2,0},{4,2},{6,4},{8,6},{10,8},{12,10},{14,12},{3,1},{5,3},{7,5},{... | collective-permute-start | bytes 49160 | tf_op jit(solution)/shard_map/ppermute | solution.py:324
  123.3 16.3 %collective-permute-start = (bf16[128,64]{0,1:T(8,128)(2,1)S(1)}, bf16[128,64]{0,1:T(8,128)(2,1)S(1)}, u32[]{:S(2)}, u32[]{:S(2)}) collective-permute-start(bf16[128,64]{0,1:T(8,128)(2,1)S(1)} %fusion.101), channel_id=1, source_target_pairs={{0,2},{2,4},{4,6},{6,8},{8,10},{10,12},{12,14},{1,3},{3,5},{5,7},{... | collective-permute-start | bytes 49160 | tf_op jit(solution)/shard_map/ppermute | solution.py:323
  127.8 9.3 %copy-start.26 = (pred[4]{0:T(512)(128)(4,1)S(1)}, pred[4]{0:T(512)(128)(4,1)}, u32[]{:S(2)}) copy-start(pred[4]{0:T(512)(128)(4,1)} %copy-done.25) | copy-start | bytes 16
  127.9 9.3 %copy-start.24 = (pred[4]{0:T(512)(128)(4,1)S(1)}, pred[4]{0:T(512)(128)(4,1)}, u32[]{:S(2)}) copy-start(pred[4]{0:T(512)(128)(4,1)} %copy-done.23) | copy-start | bytes 16
  127.9 9.3 %copy-start.19 = (f32[4,128]{1,0:T(4,128)S(1)}, f32[4,128]{1,0:T(4,128)}, u32[]{:S(2)}) copy-start(f32[4,128]{1,0:T(4,128)} %param.26) | copy-start | bytes 6148
  141.1 2.2 %copy-start.3 = (bf16[2,4,384,384]{3,2,1,0:T(8,128)(2,1)S(1)}, bf16[2,4,384,384]{3,2,1,0:T(8,128)(2,1)}, u32[]{:S(2)}) copy-start(bf16[2,4,384,384]{3,2,1,0:T(8,128)(2,1)} %copy-done.2) | copy-start | bytes 7077892
  143.3 2.1 %copy-start.4 = (f32[384,3072]{1,0:T(8,128)}, f32[384,3072]{1,0:T(8,128)S(1)}, u32[]{:S(2)}) copy-start(f32[384,3072]{1,0:T(8,128)S(1)} %multiply_add_fusion.1) | copy-start | bytes 14155780
  151.4 1.5 copy-start.11
  151.4 1.5 copy-start.12
  151.4 1.5 copy-start.13
  151.4 1.5 copy-start.14
  151.4 1.6 copy-start.15
  151.4 1.6 copy-start.18
  151.4 1.6 copy-start.29
  155.1 7.0 %copy-start.27 = (f32[128]{0:T(128)S(1)}, f32[128]{0:T(128)}, u32[]{:S(2)}) copy-start(f32[128]{0:T(128)} %get-tuple-element.37) | copy-start | bytes 1540
  155.1 7.0 %copy-start.28 = (f32[128]{0:T(128)S(1)}, f32[128]{0:T(128)}, u32[]{:S(2)}) copy-start(f32[128]{0:T(128)} %get-tuple-element.38) | copy-start | bytes 1540
  (3 other events, 3.0 us)

commit v3 on v1

--- a/solution.py
+++ b/solution.py
@@ -1,8 +1,11 @@
+import functools
 import math
 
 import jax
 import jax.numpy as jnp
 from jax import lax
+from jax.experimental import pallas as pl
+from jax.experimental.pallas import tpu as pltpu
 from jax.sharding import PartitionSpec as P
 
 GRID_W = 64
@@ -31,6 +34,207 @@
     freqs = jnp.exp(-math.log(10000.0) * index / half_width)
     angles = timestep.astype(jnp.float32)[:, None] * freqs[None, :]
     return jnp.concatenate([jnp.cos(angles), jnp.sin(angles)], axis=-1)
+
+
+MESH = pl.DeviceIdType.MESH
+NEAR = 2
+PIECES = 4
+
+
+def fold_kernel(n_group, n_seq, n_mp, pieces, fold_ref, slim_ref, mod_ref, *refs):
+    fold_out, slim_out, mod_out_ref = refs[2:5]
+    pair_refs, pair_outs = refs[:2], refs[5:7]
+    (
+        near_in, part, far_in, slim_near, slim_part, slim_far, mod_in, *pair_in,
+        near_sems, far_sems, back_sems, last_sems, mod_sems, pair_sems,
+    ) = refs[7:]
+    far = n_seq // NEAR
+    group, seq, mp = lax.axis_index("group"), lax.axis_index("seq"), lax.axis_index("mp")
+    my_far, my_near = seq // NEAR, lax.rem(seq, NEAR)
+    other = lax.rem(my_near + 1, NEAR)
+    piece = fold_ref.shape[2] // pieces
+    share = fold_ref.shape[2]
+    half = far * share
+    f32 = jnp.float32
+
+    partners = [(dg, ds) for dg in range(n_group) for ds in range(n_seq) if dg or ds]
+    barrier = pltpu.get_barrier_semaphore()
+    for dg, ds in partners:
+        target = {"group": lax.rem(group + dg, n_group), "seq": lax.rem(seq + ds, n_seq)}
+        pl.semaphore_signal(barrier, inc=1, device_id=target, device_id_type=MESH)
+    for dm in range(1, n_mp):
+        target = {"mp": lax.rem(mp + dm, n_mp)}
+        pl.semaphore_signal(barrier, inc=1, device_id=target, device_id_type=MESH)
+    pl.semaphore_wait(barrier, len(partners) + n_mp - 1)
+
+    def far_id(step):
+        return lax.rem(my_far + step, far) * NEAR + my_near
+
+    def lanes(start, size):
+        return pl.ds(pl.multiple_of(start, 128), size)
+
+    def rows(s):
+        return pl.ds((s - 1) * piece, piece)
+
+    def source(s, near):
+        return slim_ref.at[:, lanes(near * half, half)] if s == 0 else fold_ref.at[near, :, rows(s)]
+
+    def from_near(s):
+        return slim_near if s == 0 else near_in.at[:, rows(s)]
+
+    def partial(s):
+        return slim_part if s == 0 else part.at[:, rows(s)]
+
+    def partial_of(s, z):
+        return slim_part.at[:, lanes(z * share, share)] if s == 0 else part.at[z, rows(s)]
+
+    def from_far(s, k):
+        return slim_far.at[k - 1] if s == 0 else far_in.at[k - 1, rows(s)]
+
+    def result_of(s):
+        if s == 0:
+            return slim_out.at[:, lanes(my_near * half + my_far * share, share)]
+        return fold_out.at[my_near, my_far, rows(s)]
+
+    def result(s):
+        if s == 0:
+            return slim_out.at[:, lanes(my_near * half, half)]
+        return fold_out.at[my_near, :, rows(s)]
+
+    def send(src, dst, sems, index, target):
+        copy = pltpu.make_async_remote_copy(
+            src_ref=src,
+            dst_ref=dst,
+            send_sem=sems.at[(0, *index)],
+            recv_sem=sems.at[(1, *index)],
+            device_id=target,
+            device_id_type=MESH,
+        )
+        copy.start()
+        return copy
+
+    count = pieces + 1
+    across = {"seq": my_far * NEAR + other}
+    near_copies = [
+        send(source(s, other), from_near(s), near_sems, (s,), across) for s in range(count)
+    ]
+    mod_copies = []
+    for dg, ds in partners:
+        to_group = lax.rem(group + dg, n_group)
+        target = {"group": to_group, "seq": lax.rem(seq + ds, n_seq)}
+        mod_copies.append(
+            send(mod_ref.at[to_group], mod_in.at[dg, ds], mod_sems, (dg, ds), target)
+        )
+    pair_copies = [
+        send(pair_refs[i], pair_in[i].at[dm], pair_sems, (i, dm), {"mp": lax.rem(mp + dm, n_mp)})
+        for i in range(2)
+        for dm in range(1, n_mp)
+    ]
+
+    far_copies, back_copies, last_copies = {}, {}, {}
+    for s in range(count):
+        near_copies[s].wait_recv()
+        partial(s)[...] = (
+            source(s, my_near)[...].astype(f32) + from_near(s)[...].astype(f32)
+        ).astype(part.dtype)
+        for k in range(1, far):
+            far_copies[s, k] = send(
+                partial_of(s, lax.rem(my_far + k, far)),
+                from_far(s, k),
+                far_sems,
+                (s, k - 1),
+                {"seq": far_id(k)},
+            )
+
+    def finish(s):
+        for k in range(1, far):
+            back_copies[s, k].wait_recv()
+        last_copies[s] = send(result(s), result(s), last_sems, (s,), across)
+
+    for s in range(count):
+        total = partial_of(s, my_far)[...].astype(f32)
+        for k in range(1, far):
+            far_copies[s, k].wait_recv()
+            total = total + from_far(s, k)[...].astype(f32)
+        result_of(s)[...] = total.astype(fold_out.dtype)
+        for k in range(1, far):
+            back_copies[s, k] = send(
+                result_of(s), result_of(s), back_sems, (s, k - 1), {"seq": far_id(k)}
+            )
+        if s >= 1:
+            finish(s - 1)
+    for copy in mod_copies + pair_copies:
+        copy.wait_recv()
+    for dg in range(n_group):
+        total = mod_ref[group] if dg == 0 else mod_in[dg, 0]
+        for ds in range(1, n_seq):
+            total = total + mod_in[dg, ds]
+        mod_out_ref[lax.rem(group + n_group - dg, n_group)] = total
+    for i in range(2):
+        total = pair_refs[i][...]
+        for dm in range(1, n_mp):
+            total = total + pair_in[i][dm]
+        pair_outs[i][...] = total
+    finish(pieces)
+    for s in range(count):
+        last_copies[s].wait_recv()
+    for copies in (near_copies, far_copies.values(), back_copies.values(), last_copies.values()):
+        for copy in copies:
+            copy.wait_send()
+    for copy in mod_copies + pair_copies:
+        copy.wait_send()
+
+
+def summed_folds(fold, slim, mod, pair):
+    n_group, n_seq, n_mp = (lax.axis_size(axis) for axis in ("group", "seq", "mp"))
+    hidden, columns = fold.shape
+    share = hidden // n_seq
+    far = n_seq // NEAR
+    mod_rows = mod.shape[1] // 128
+    fits = hidden % n_seq == 0 and n_seq % NEAR == 0 and far > 1 and share % (16 * PIECES) == 0
+    if not fits or share % 128 or mod.shape[1] % 128 or mod.shape[0] != n_group:
+        halves = lax.all_gather(lax.psum(mod, "seq"), "group", axis=1)
+        own = lax.dynamic_slice_in_dim(halves, lax.axis_index("group"), 1, 0)[0]
+        return lax.psum(fold, "seq"), lax.psum(slim, "seq"), own, lax.psum(pair, "mp")
+    dma = pltpu.SemaphoreType.DMA
+    vmem = pl.BlockSpec(memory_space=pltpu.VMEM)
+    tall, kind, height = PIECES + 1, fold.dtype, slim.shape[0]
+    summed, slim_sum, own, *pair_sum = pl.pallas_call(
+        functools.partial(fold_kernel, n_group, n_seq, n_mp, PIECES),
+        out_shape=(
+            jax.ShapeDtypeStruct((NEAR, far, share, columns), kind),
+            jax.ShapeDtypeStruct(slim.shape, kind),
+            jax.ShapeDtypeStruct((n_group, mod_rows, 128), jnp.float32),
+            *(jax.ShapeDtypeStruct(value.shape, value.dtype) for value in pair),
+        ),
+        in_specs=[vmem] * 5,
+        out_specs=(vmem,) * 5,
+        scratch_shapes=[
+            pltpu.VMEM((far, share, columns), kind),
+            pltpu.VMEM((far, share, columns), kind),
+            pltpu.VMEM((far - 1, share, columns), kind),
+            pltpu.VMEM((height, far * share), kind),
+            pltpu.VMEM((height, far * share), kind),
+            pltpu.VMEM((far - 1, height, share), kind),
+            pltpu.VMEM((n_group, n_seq, mod_rows, 128), jnp.float32),
+            *(pltpu.VMEM((n_mp, *value.shape), value.dtype) for value in pair),
+            dma((2, tall)),
+            dma((2, tall, far - 1)),
+            dma((2, tall, far - 1)),
+            dma((2, tall)),
+            dma((2, n_group, n_seq)),
+            dma((2, 2, n_mp)),
+        ],
+        compiler_params=pltpu.CompilerParams(
+            collective_id=0, has_side_effects=True, vmem_limit_bytes=40 * 1024 * 1024
+        ),
+    )(
+        fold.reshape(NEAR, far, share, columns),
+        slim,
+        mod.reshape(mod.shape[0], mod_rows, 128),
+        *pair,
+    )
+    return summed.reshape(hidden, columns), slim_sum, own.reshape(n_group, mod.shape[1]), pair_sum
 
 
 def shifted(grid, offset):
@@ -111,11 +315,9 @@
         ],
         axis=1,
     ).reshape(chunk, picked * channels)
-    own_proj = jnp.where(lax.axis_index("mp") == owner, own_proj, jnp.zeros_like(own_proj))
-    proj_chunk = lax.psum(own_proj, "mp")
-    out_fold = lax.psum(
-        jnp.dot(down_weight, proj_chunk, preferred_element_type=f32).astype(bf16), "seq"
-    )
+    own_proj = lax.all_gather(own_proj, "mp")
+    proj_chunk = lax.dynamic_index_in_dim(own_proj, owner, 0, keepdims=False)
+    out_terms = jnp.dot(down_weight, proj_chunk, preferred_element_type=f32).astype(bf16)
     embed_f = embed_full.astype(f32)
     embed_centered = embed_f - jnp.mean(embed_f, axis=1, keepdims=True)
     gram = jnp.einsum("cd,ed->ce", embed_centered, embed_centered, precision=highest)
@@ -123,23 +325,23 @@
         [embed_centered * (1.0 + tmod[1:2]), tmod[0:1]], axis=0
     ).astype(bf16)
     stacked = lax.dynamic_slice_in_dim(stacked, start, chunk, 1)
-    in_fold = lax.psum(
-        jnp.dot(stacked, up_weight, preferred_element_type=f32).astype(bf16), "seq"
-    )
-    embed_proj = lax.psum(
-        jnp.einsum("cd,kdh->kch", teacher_embed, head_proj, preferred_element_type=f32), "mp"
-    )
+    pad = -stacked.shape[0] % 16
+    stacked = jnp.pad(stacked, ((0, pad), (0, 0)))
+    in_terms = jnp.dot(stacked, up_weight, preferred_element_type=f32).astype(bf16)
+    embed_proj = jnp.einsum("cd,kdh->kch", teacher_embed, head_proj, preferred_element_type=f32)
 
     hidden = student_hidden[0].astype(f32)
-    first_sum, square_sum = lax.psum((jnp.sum(hidden, -1), jnp.sum(hidden * hidden, -1)), "mp")
-    tok_mean = (first_sum / width)[:, None]
-    tok_var = (square_sum / width)[:, None] - tok_mean * tok_mean
+    token_sums = jnp.stack([jnp.sum(hidden, -1), jnp.sum(hidden * hidden, -1)])
     half_mod = jnp.einsum(
         "sk,kjd->sjd", student_cond, student_mod.astype(f32), precision=highest
     )
-    half_mod = lax.psum(half_mod, "seq")
-    halves_all = lax.all_gather(half_mod, "group", axis=1, tiled=True)
-    own_mod = lax.dynamic_slice_in_dim(halves_all, lax.axis_index("group"), 1, 0)[0]
+    out_fold, in_fold, own_mod, (token_sums, embed_proj) = summed_folds(
+        out_terms, in_terms, half_mod[:, 0], (token_sums, embed_proj)
+    )
+    up_fold = in_fold[:latent_width]
+    bias = in_fold[latent_width : latent_width + 1].astype(f32)
+    tok_mean = (token_sums[0] / width)[:, None]
+    tok_var = (token_sums[1] / width)[:, None] - tok_mean * tok_mean
     normed = (
         (hidden - tok_mean) * lax.rsqrt(tok_var + EPSILON) * (1.0 + own_mod[1:2]) + own_mod[0:1]
     ).astype(bf16)
@@ -161,13 +363,10 @@
     wide_gram = jnp.dot(wide_f, gram, precision=highest)
     var_t = jnp.sum(wide_f * wide_gram, -1, keepdims=True) / width
     inv_std = lax.rsqrt(var_t + EPSILON)
-    up_fold = in_fold[:latent_width]
-    bias = in_fold[latent_width:].astype(f32)
     preact = inv_std * jnp.dot(wide, up_fold, preferred_element_type=f32) + bias
     activated = gelu_tanh(preact).astype(bf16)
-    block_terms = lax.psum(
-        jnp.dot(activated, out_fold, preferred_element_type=f32).astype(bf16), "mp"
-    ).astype(f32)
+    block_terms = jnp.dot(activated, out_fold, preferred_element_type=f32).astype(bf16)
+    block_terms = jnp.sum(lax.all_gather(block_terms, "mp").astype(f32), axis=0)
     projected = jnp.einsum("tc,kch->kth", wide_f, embed_proj, precision=highest)
     projected = projected + sum(
         one_hot[:, j][:, None, None]

time: 213 us -> 144 us (0.68)
  waiting for transfers between devices: 85.4 us -> 0.01 us
  Pallas kernels: 0 us -> 68.1 us
  blocking collectives: 56.2 us -> 15.2 us
  between operations: 18.7 us -> 6.03 us
  local copies, waits for them, and re-layouts: 9.95 us -> 16.9 us
  matrix products: 26.3 us -> 21 us
  starting transfers between devices: 2.75 us -> 5.83 us
  other arithmetic: 12.6 us -> 9.95 us
    psum x4 -> x0, waiting for transfers between devices: 81.8 us -> none  [the longest x1 40.4 us: per_device(): lax.psum(jnp.dot(down_weight, proj_chunk, preferred_element_type=f32).ast...]
    pallas_call x0 -> x1, Pallas kernels: none -> 68.1 us  [summed_folds(): pl.pallas_call(functools.partial(fold_kernel, n_group, n_seq, n_mp, PIECE...]
    psum x2 -> x0, blocking collectives: 40.8 us -> none  [the longest x1 38.4 us: per_device(): half_mod = lax.psum(half_mod, 'seq')]
    ppermute x1, waiting for transfers between devices: 3.55 us -> 0.01 us  [per_device(): after = lax.ppermute(noised[:halo], 'seq', downs)]
    ppermute x1, starting transfers between devices: 1.29 us -> 4.55 us  [per_device(): before = lax.ppermute(noised[tokens - halo:], 'seq', ups)]
    convert_element_type x0 -> x1, local copies, waits for them, and re-layouts: none -> 2.6 us  [per_device(): jnp.dot(down_weight, proj_chunk, preferred_element_type=f32).astype(bf16)]
    unnamed x58 -> x97, local copies, waits for them, and re-layouts: 4.79 us -> 6.51 us
    all_gather x1 -> x2, blocking collectives: 4.39 us -> 4.36 us  [the longest x1 2.27 us: per_device(): block_terms = jnp.sum(lax.all_gather(block_terms, 'mp').astype(f32), axis=0)]
  transfers between devices with their start and end apart: 6 -> 2, of which waited for: 5 -> 0; matrix products, arithmetic and copies ran while one was open for 9% -> 2% of each run, Pallas kernels for 0% -> 0%
where the time goes in v3:
time: 144 us; the launch traced here: 143 us
  Pallas kernels  68.1 us (47%)
  matrix products  21 us (15%)
  local copies, waits for them, and re-layouts  16.9 us (12%)
  blocking collectives  15.2 us (11%)
  other arithmetic  9.95 us (7%)
  between operations  6.03 us (4%)
  starting transfers between devices  5.83 us (4%)
    pallas_call x1, Pallas kernels, summed_folds(): pl.pallas_call(functools.partial(fold_kernel, n_group, n_seq, n_mp, PIECE...  68.1 us
    unnamed x97, local copies, waits for them, and re-layouts  6.51 us
    ppermute x1, starting transfers between devices, per_device(): before = lax.ppermute(noised[tokens - halo:], 'seq', ups)  4.55 us
    psum x1, blocking collectives, per_device(): lax.psum(lax.dot_general(preact_grad, up_fold, (((1,), (1,)), ((), ())),...  3.41 us
    psum x1, blocking collectives, per_device(): lax.psum(jnp.dot(normed, student_out, preferred_element_type=f32).astype(...  3.36 us
    dot_general x1, matrix products, per_device(): lax.dot_general(preact_grad, up_fold, (((1,), (1,)), ((), ())), preferred...  3.3 us
  transfers between devices with their start and end apart: 2, of which 0 were waited for; matrix products, arithmetic and copies ran while one was open for 2% of the time, Pallas kernels for 0%

profile of v3, /device:TPU:0, one launch (start us, length us, event | category | flops | bytes accessed | tf_op | source)
XLA Modules:
  0.0 143.0 jit_solution(18054613803721764994)
XLA Ops:
  0.7 0.8 fusion.105
  1.6 1.2 convert_convert_fusion.1
  7.5 2.1 %fusion.14 = f32[1,2,1536]{2,0,1:T(1,128)S(1)} fusion(bf16[256,2,1536]{2,1,0:T(2,128)(2,1)} %param.21, f32[1,128]{1,0:T(1,128)S(1)} %get-tuple-element.49, f32[1,128]{1,0:T(1,128)S(1)} %get-tuple-element.50), kind=kOutput, calls=%fused_computation.20 | convolution fusion | flops 9437440 | bytes 1586176 | tf_op jit(solution)/shard_map/f,fjd->jd/dot_general | solution.py:300
  9.7 1.9 %all_gather.17 = f32[2,3072]{1,0:T(2,128)S(1)} all-gather(f32[2,1536]{1,0:T(2,128)S(1)} %bitcast.145), channel_id=1, replica_groups=mesh['group'=2,'seq'=8,'mp'=2] {'mp'}, dimensions={1}, use_global_device_ids=true | all-gather | bytes 36864 | tf_op jit(solution)/shard_map/all_gather | solution.py:306
  11.9 2.1 %all_gather.16 = bf16[64,3072]{1,0:T(8,128)(2,1)S(1)} all-gather(bf16[64,1536]{1,0:T(8,128)(2,1)S(1)} %copy-done.8), channel_id=1, replica_groups=mesh['group'=2,'seq'=8,'mp'=2] {'mp'}, dimensions={1}, use_global_device_ids=true | all-gather | bytes 589824 | tf_op jit(solution)/shard_map/all_gather | solution.py:299
  15.7 1.0 constant_dynamic-slice_fusion.1
  17.1 2.1 %all_gather.15 = bf16[2,384,256]{2,1,0:T(8,128)(2,1)S(1)} all-gather(bf16[1,384,256]{2,1,0:T(8,128)(2,1)S(1)} %copy.38), channel_id=1, replica_groups=mesh['group'=2,'seq'=8,'mp'=2] {'mp'}, dimensions={0}, use_global_device_ids=true | all-gather | bytes 589824 | tf_op jit(solution)/shard_map/all_gather | solution.py:318
  19.2 2.2 %fusion.5 = bf16[3072,256]{0,1:T(8,128)(2,1)} fusion(bf16[3072,384]{1,0:T(8,128)(2,1)S(1)} %copy-done, bf16[2,384,256]{2,1,0:T(8,128)(2,1)S(1)} %all_gather.15, s32[]{:T(128)S(6)} %select_n.40), kind=kOutput, calls=%fused_computation.9 | convolution fusion | flops 604766208 | bytes 4128772 | tf_op jit(solution)/shard_map/dot_general | solution.py:320
  21.4 2.6 %copy.39 = bf16[3072,256]{1,0:T(8,128)(2,1)} copy(bf16[3072,256]{0,1:T(8,128)(2,1)} %fusion.5) | data formatting | bytes 3145728 | tf_op jit(solution)/shard_map/convert_element_type | solution.py:320
  24.2 2.4 %copy.40 = bf16[384,1,1536]{0,2,1:T(8,128)(2,1)} copy(bf16[384,1,1536]{2,0,1:T(8,128)(2,1)} %param.16) | data formatting | bytes 2359296 | tf_op args[2]
  26.6 2.3 %fusion.95 = f32[2,12,128]{2,0,1:T(2,128)S(1)} fusion(bf16[12,128,384]{2,1,0:T(8,128)(2,1)} %bitcast.137, f32[2,384]{1,0:T(2,128)S(1)} %copy-done.36), kind=kOutput, calls=%fused_computation.142 | convolution fusion | flops 14155776 | bytes 1195008 | tf_op jit(solution)/shard_map/sk,kjd->sjd/dot_general | solution.py:335
  29.1 2.3 %convolution_convert_fusion.1.slim_ref = bf16[80,3072]{1,0:T(8,128)(2,1)S(1)} fusion(bf16[384,3072]{1,0:T(8,128)(2,1)} %param.22, bf16[65,384]{1,0:T(8,128)(2,1)S(1)} %fusion.88), kind=kOutput, calls=%fused_computation.11 | convolution fusion | flops 188989440 | bytes 2900736 | tf_op jit(solution)/shard_map/dot_general | solution.py:330
  31.5 68.1 %shard_map.157 = (bf16[2,4,384,256]{3,2,1,0:T(8,128)(2,1)S(1)}, bf16[80,3072]{1,0:T(8,128)(2,1)S(1)}, f32[2,12,128]{2,1,0:T(8,128)S(1)}, f32[2,128]{1,0:T(2,128)S(1)}, f32[4,64,128]{2,1,0:T(8,128)S(1)}) custom-call(bf16[2,4,384,256]{3,2,1,0:T(8,128)(2,1)S(1)} %bitcast.134, bf16[80,3072]{1,0:T(8,128)(2,1)S(1)} %convolution_convert_fusion.1.slim_ref, ...), custom_call_target="tpu_custom_call" | custom-call | tf_op jit(solution)/shard_map/pallas_call | solution.py:202
  99.6 1.2 copy-done.2
  101.2 3.4 %psum.14 = bf16[128,64]{0,1:T(8,128)(2,1)S(1)} all-reduce(bf16[128,64]{0,1:T(8,128)(2,1)S(1)} %convolution_convert_fusion.2), channel_id=1, replica_groups=mesh['group'=2,'seq'=8,'mp'=2] {'mp'}, use_global_device_ids=true, to_apply=%region_6.7 | all-reduce | flops 8192 | bytes 32768 | tf_op jit(solution)/shard_map/psum | solution.py:348
  105.2 1.3 collective-permute-start.1
  106.5 4.5 %collective-permute-start = (bf16[128,64]{0,1:T(8,128)(2,1)S(1)}, bf16[128,64]{0,1:T(8,128)(2,1)S(1)}, u32[]{:S(2)}, u32[]{:S(2)}) collective-permute-start(bf16[128,64]{0,1:T(8,128)(2,1)S(1)} %fusion.94), channel_id=1, source_target_pairs={{0,2},{2,4},{4,6},{6,8},{8,10},{10,12},{12,14},{1,3},{3,5},{5,7},{... | collective-permute-start | bytes 49160 | tf_op jit(solution)/shard_map/ppermute | solution.py:358
  111.0 1.7 %fusion.26 = f32[64,64]{1,0:T(8,128)S(1)} fusion(bf16[64,3072]{1,0:T(8,128)(2,1)S(1)} %all_gather.16, f32[64]{0:T(128)} %copy-done.46), kind=kOutput, calls=%fused_computation.38 | convolution fusion | flops 151388160 | bytes 409856 | tf_op jit(solution)/shard_map/cd,ed->ce/dot_general | solution.py:323
  114.7 0.9 multiply_reduce_fusion.2
  116.2 0.8 multiply_add_fusion.1
  117.6 1.6 %fusion.18 = bf16[384,256]{1,0:T(8,128)(2,1)S(1)} fusion(bf16[3072,256]{1,0:T(8,128)(2,1)S(1)} %bitcast.136, f32[384,3072]{1,0:T(8,128)S(1)} %multiply_add_fusion.1), kind=kOutput, calls=%fused_computation.25 | convolution fusion | flops 614694912 | bytes 6488064 | tf_op jit(solution)/shard_map/dot_general | solution.py:368
  119.2 2.3 %all-gather = bf16[768,256]{1,0:T(8,128)(2,1)S(1)} all-gather(bf16[384,256]{1,0:T(8,128)(2,1)S(1)} %fusion.18), channel_id=2, replica_groups=mesh['group'=2,'seq'=8,'mp'=2] {'mp'}, dimensions={0}, use_global_device_ids=true | all-gather | bytes 589824 | tf_op jit(solution)/shard_map/all_gather | solution.py:369
  122.4 1.1 copy.42
  123.4 1.5 %fusion.16 = f32[4,384,128]{1,2,0:T(8,128)} fusion(f32[4,64,128]{2,1,0:T(8,128)S(1)} %get-tuple-element.10, f32[384,128]{0,1:T(8,128)S(1)} %copy.43, f32[4]{0:T(128)S(1)} %convert_element_type.156, f32[384,128]{0,1:T(8,128)S(1)} %copy.42, f32[4]{0:T(128)S(1)} %convert_element_type.151, bf16[128,64]{0,1:T(8,128)(2,1)S(1)} %collective-permute-done.1, ...), kind=kOutput, calls=%fused_computation.23 | convolution fusion | flops 151928832 | bytes 1359904 | tf_op jit(solution)/shard_map/tc,kch->kth/dot_general | solution.py:370
  124.9 2.3 %copy.44 = f32[4,384,128]{2,1,0:T(8,128)} copy(f32[4,384,128]{1,2,0:T(8,128)} %fusion.16) | data formatting | bytes 1572864 | tf_op jit(solution)/shard_map/add | solution.py:371
  127.2 1.3 broadcast_multiply_fusion
  130.1 0.8 fusion.77
  130.8 1.3 reshape.200
  132.9 1.6 %multiply_reduce_fusion.1 = (bf16[2,64,128]{2,1,0:T(8,128)(2,1)}, bf16[2,64,128]{2,1,0:T(8,128)(2,1)}, bf16[4,2,64,128]{3,2,1,0:T(8,128)(2,1)}) fusion(bf16[4]{0:T(256)(128)(2,1)S(1)} %copy-done.37, bf16[4]{0:T(256)(128)(2,1)S(1)} %copy-done.38, f32[4,128]{1,0:T(4,128)S(1)} %copy-done.28, f32[4,4,64,128]{3,2,1,0:T(8,128)S(1)} %get-tuple-element.20, ...), kind=kLoop, calls=%fused_computation.119 | loop fusion | flops 1409024 | bytes 2033680 | tf_op jit(solution)/shard_map/reduce_sum | solution.py:391
  134.5 3.3 %fusion.17 = f32[128,64]{0,1:T(8,128)S(1)} fusion(bf16[3072,256]{1,0:T(8,128)(2,1)} %bitcast.135, f32[384,3072]{1,0:T(8,128)} %copy-done.4, bf16[80,3072]{1,0:T(8,128)(2,1)S(1)} %get-tuple-element.11, bf16[128,128]{1,0:T(8,128)(2,1)} %bitcast.149, bf16[128,128]{1,0:T(8,128)(2,1)} %bitcast.148), kind=kOutput, calls=%fused_computation.24 | convolution fusion | flops 259260416 | bytes 3637248 | tf_op jit(solution)/shard_map/dot_general | solution.py:402
  137.8 3.4 %psum.15 = f32[128,64]{0,1:T(8,128)S(1)} all-reduce(f32[128,64]{0,1:T(8,128)S(1)} %fusion.17), channel_id=1, replica_groups=mesh['group'=2,'seq'=8,'mp'=2] {'mp'}, use_global_device_ids=true, to_apply=%region_12.13 | all-reduce | flops 8192 | bytes 65536 | tf_op jit(solution)/shard_map/psum | solution.py:401
  141.3 1.6 %fusion.23 = f32[1,128,64]{1,2,0:T(8,128)} fusion(bf16[4,128,128]{2,1,0:T(8,128)(2,1)S(1)} %bitcast.141, f32[4,64,128]{2,1,0:T(8,128)S(1)} %get-tuple-element.10, f32[128,64]{0,1:T(8,128)S(1)} %psum.15, f32[384,64]{0,1:T(8,128)} %get-tuple-element.46, f32[128]{0:T(128)S(1)} %copy-done.44, f32[128]{0:T(128)S(1)} %broadcast_multiply_fusion.1, ...), kind=kOutput, calls=%fused_computation.30 | convolution fusion | flops 50380800 | bytes 361988 | tf_op jit(solution)/shard_map/kth,kch->tc/dot_general | solution.py:388
  (141 shorter events, 10.1 us)
Async XLA Ops:
  0.6 18.6 %copy-start = (bf16[3072,384]{1,0:T(8,128)(2,1)S(1)}, bf16[3072,384]{1,0:T(8,128)(2,1)}, u32[]{:S(2)}) copy-start(bf16[3072,384]{1,0:T(8,128)(2,1)} %param.23) | copy-start | bytes 7077892
  0.6 11.0 %copy-start.6 = (bf16[1,128,1536]{2,1,0:T(8,128)(2,1)S(1)}, bf16[1,128,1536]{2,1,0:T(8,128)(2,1)}, u32[]{:S(2)}) copy-start(bf16[1,128,1536]{2,1,0:T(8,128)(2,1)} %param.14) | copy-start | bytes 1179652
  0.7 11.3 %copy-start.8 = (bf16[64,1536]{1,0:T(8,128)(2,1)S(1)}, bf16[64,1536]{1,0:T(8,128)(2,1)}, u32[]{:S(2)}) copy-start(bf16[64,1536]{1,0:T(8,128)(2,1)} %param.20) | copy-start | bytes 589828
  2.9 1.2 copy-start.41
  6.7 7.4 %copy-start.5 = (bf16[4,1536,128]{2,1,0:T(8,128)(2,1)S(1)}, bf16[4,1536,128]{2,1,0:T(8,128)(2,1)}, u32[]{:S(2)}) copy-start(bf16[4,1536,128]{2,1,0:T(8,128)(2,1)} %param.24) | copy-start | bytes 4718596
  24.0 2.6 %copy-start.36 = (f32[2,384]{1,0:T(2,128)S(1)}, f32[2,384]{1,0:T(2,128)}, u32[]{:S(2)}) copy-start(f32[2,384]{1,0:T(2,128)} %param.15) | copy-start | bytes 9220
  24.2 4.7 %copy-start.46 = (f32[64]{0:T(128)}, f32[64]{0:T(128)S(1)}, u32[]{:S(2)}) copy-start(f32[64]{0:T(128)S(1)} %broadcast_multiply_fusion.2) | copy-start | bytes 772
  29.0 2.4 %copy-start.1 = (bf16[3072,256]{1,0:T(8,128)(2,1)S(1)}, bf16[3072,256]{1,0:T(8,128)(2,1)}, u32[]{:S(2)}) copy-start(bf16[3072,256]{1,0:T(8,128)(2,1)} %copy.39) | copy-start | bytes 4718596
  31.4 69.4 %copy-start.7 = (bf16[1,128,1536]{2,1,0:T(8,128)(2,1)S(1)}, bf16[1,128,1536]{2,1,0:T(8,128)(2,1)}, u32[]{:S(2)}) copy-start(bf16[1,128,1536]{2,1,0:T(8,128)(2,1)} %param.14) | copy-start | bytes 1179652
  31.4 69.4 %copy-start.47 = (bf16[1536,64]{0,1:T(8,128)(2,1)S(1)}, bf16[1536,64]{0,1:T(8,128)(2,1)}, u32[]{:S(2)}) copy-start(bf16[1536,64]{0,1:T(8,128)(2,1)} %param.17) | copy-start | bytes 589828
  31.5 73.1 %copy-start.32 = (bf16[1,128,64]{1,2,0:T(8,128)(2,1)S(1)}, bf16[1,128,64]{1,2,0:T(8,128)(2,1)}, u32[]{:S(2)}) copy-start(bf16[1,128,64]{1,2,0:T(8,128)(2,1)} %param.19) | copy-start | bytes 49156
  99.6 1.2 copy-start.2
  100.8 12.6 %copy-start.31 = (f32[4,3,3,128]{3,0,2,1:T(4,128)S(1)}, f32[4,3,3,128]{3,0,2,1:T(4,128)}, u32[]{:S(2)}) copy-start(f32[4,3,3,128]{3,0,2,1:T(4,128)} %param.25) | copy-start | bytes 55300
  100.8 13.2 %copy-start.42 = (pred[4]{0:T(512)(128)(4,1)S(1)}, pred[4]{0:T(512)(128)(4,1)}, u32[]{:S(2)}) copy-start(pred[4]{0:T(512)(128)(4,1)} %copy-done.41) | copy-start | bytes 16
  100.8 13.3 %copy-start.40 = (pred[4]{0:T(512)(128)(4,1)S(1)}, pred[4]{0:T(512)(128)(4,1)}, u32[]{:S(2)}) copy-start(pred[4]{0:T(512)(128)(4,1)} %copy-done.39) | copy-start | bytes 16
  100.8 13.3 %copy-start.34 = (f32[4,128]{1,0:T(4,128)S(1)}, f32[4,128]{1,0:T(4,128)}, u32[]{:S(2)}) copy-start(f32[4,128]{1,0:T(4,128)} %param.26) | copy-start | bytes 6148
  105.2 9.5 %collective-permute-start.1 = (bf16[128,64]{0,1:T(8,128)(2,1)S(1)}, bf16[128,64]{0,1:T(8,128)(2,1)S(1)}, u32[]{:S(2)}, u32[]{:S(2)}) collective-permute-start(bf16[128,64]{0,1:T(8,128)(2,1)S(1)} %fusion.94), channel_id=1, source_target_pairs={{2,0},{4,2},{6,4},{8,6},{10,8},{12,10},{14,12},{3,1},{5,3},{7,5},{... | collective-permute-start | bytes 49160 | tf_op jit(solution)/shard_map/ppermute | solution.py:359
  106.5 8.2 %collective-permute-start = (bf16[128,64]{0,1:T(8,128)(2,1)S(1)}, bf16[128,64]{0,1:T(8,128)(2,1)S(1)}, u32[]{:S(2)}, u32[]{:S(2)}) collective-permute-start(bf16[128,64]{0,1:T(8,128)(2,1)S(1)} %fusion.94), channel_id=1, source_target_pairs={{0,2},{2,4},{4,6},{6,8},{8,10},{10,12},{12,14},{1,3},{3,5},{5,7},{... | collective-permute-start | bytes 49160 | tf_op jit(solution)/shard_map/ppermute | solution.py:358
  114.6 2.3 %copy-start.10 = (bf16[128,64]{0,1:T(8,128)(2,1)}, bf16[128,64]{0,1:T(8,128)(2,1)S(1)}, u32[]{:S(2)}) copy-start(bf16[128,64]{0,1:T(8,128)(2,1)S(1)} %collective-permute-done) | copy-start | bytes 49156
  116.2 1.4 copy-start.3
  117.0 2.2 %copy-start.4 = (f32[384,3072]{1,0:T(8,128)}, f32[384,3072]{1,0:T(8,128)S(1)}, u32[]{:S(2)}) copy-start(f32[384,3072]{1,0:T(8,128)S(1)} %multiply_add_fusion.1) | copy-start | bytes 14155780
  119.2 4.2 %copy-start.11 = (bf16[128,64]{0,1:T(8,128)(2,1)S(1)}, bf16[128,64]{0,1:T(8,128)(2,1)}, u32[]{:S(2)}) copy-start(bf16[128,64]{0,1:T(8,128)(2,1)} %copy-done.10) | copy-start | bytes 49156
  128.5 0.7 copy-start.17
  128.6 0.7 copy-start.33
  129.3 0.8 copy-start.35
  132.2 0.7 copy-start.18
  132.2 0.7 copy-start.20
  132.2 0.7 copy-start.22
  132.2 0.7 copy-start.30
  134.5 6.8 %copy-start.9 = (bf16[4,2,64,128]{3,2,1,0:T(8,128)(2,1)S(1)}, bf16[4,2,64,128]{3,2,1,0:T(8,128)(2,1)}, u32[]{:S(2)}) copy-start(bf16[4,2,64,128]{3,2,1,0:T(8,128)(2,1)} %get-tuple-element.15) | copy-start | bytes 393220
  134.5 6.8 %copy-start.43 = (f32[128]{0:T(128)S(1)}, f32[128]{0:T(128)}, u32[]{:S(2)}) copy-start(f32[128]{0:T(128)} %get-tuple-element.41) | copy-start | bytes 1540
  134.5 6.8 %copy-start.44 = (f32[128]{0:T(128)S(1)}, f32[128]{0:T(128)}, u32[]{:S(2)}) copy-start(f32[128]{0:T(128)} %get-tuple-element.42) | copy-start | bytes 1540
  (18 other events, 11.9 us)

commit v4 on v3

--- a/solution.py
+++ b/solution.py
@@ -38,7 +38,7 @@
 
 MESH = pl.DeviceIdType.MESH
 NEAR = 2
-PIECES = 4
+PIECES = 8
 
 
 def fold_kernel(n_group, n_seq, n_mp, pieces, fold_ref, slim_ref, mod_ref, *refs):
@@ -114,10 +114,11 @@
         return copy
 
     count = pieces + 1
+    order = [*range(1, pieces // 2 + 1), 0, *range(pieces // 2 + 1, count)]
     across = {"seq": my_far * NEAR + other}
-    near_copies = [
-        send(source(s, other), from_near(s), near_sems, (s,), across) for s in range(count)
-    ]
+    near_copies = {
+        s: send(source(s, other), from_near(s), near_sems, (s,), across) for s in order
+    }
     mod_copies = []
     for dg, ds in partners:
         to_group = lax.rem(group + dg, n_group)
@@ -132,7 +133,7 @@
     ]
 
     far_copies, back_copies, last_copies = {}, {}, {}
-    for s in range(count):
+    for s in order:
         near_copies[s].wait_recv()
         partial(s)[...] = (
             source(s, my_near)[...].astype(f32) + from_near(s)[...].astype(f32)
@@ -151,7 +152,7 @@
             back_copies[s, k].wait_recv()
         last_copies[s] = send(result(s), result(s), last_sems, (s,), across)
 
-    for s in range(count):
+    for place, s in enumerate(order):
         total = partial_of(s, my_far)[...].astype(f32)
         for k in range(1, far):
             far_copies[s, k].wait_recv()
@@ -161,8 +162,8 @@
             back_copies[s, k] = send(
                 result_of(s), result_of(s), back_sems, (s, k - 1), {"seq": far_id(k)}
             )
-        if s >= 1:
-            finish(s - 1)
+        if place >= 1:
+            finish(order[place - 1])
     for copy in mod_copies + pair_copies:
         copy.wait_recv()
     for dg in range(n_group):
@@ -175,10 +176,10 @@
         for dm in range(1, n_mp):
             total = total + pair_in[i][dm]
         pair_outs[i][...] = total
-    finish(pieces)
-    for s in range(count):
+    finish(order[-1])
+    for s in order:
         last_copies[s].wait_recv()
-    for copies in (near_copies, far_copies.values(), back_copies.values(), last_copies.values()):
+    for copies in (near_copies.values(), far_copies.values(), back_copies.values(), last_copies.values()):
         for copy in copies:
             copy.wait_send()
     for copy in mod_copies + pair_copies:

time: 144 us -> 144 us (level)
  no operation moved by 1% of the time
where the time goes in v4:
time: 144 us; the launch traced here: 143 us
  Pallas kernels  67.9 us (47%)
  matrix products  21 us (15%)
  local copies, waits for them, and re-layouts  16.9 us (12%)
  blocking collectives  15.2 us (11%)
  other arithmetic  9.95 us (7%)
  between operations  6.03 us (4%)
  starting transfers between devices  5.83 us (4%)
    pallas_call x1, Pallas kernels, summed_folds(): pl.pallas_call(functools.partial(fold_kernel, n_group, n_seq, n_mp, PIECE...  67.9 us
    unnamed x97, local copies, waits for them, and re-layouts  6.51 us
    ppermute x1, starting transfers between devices, per_device(): before = lax.ppermute(noised[tokens - halo:], 'seq', ups)  4.55 us
    psum x1, blocking collectives, per_device(): lax.psum(lax.dot_general(preact_grad, up_fold, (((1,), (1,)), ((), ())),...  3.41 us
    psum x1, blocking collectives, per_device(): lax.psum(jnp.dot(normed, student_out, preferred_element_type=f32).astype(...  3.36 us
    dot_general x1, matrix products, per_device(): lax.dot_general(preact_grad, up_fold, (((1,), (1,)), ((), ())), preferred...  3.3 us
  transfers between devices with their start and end apart: 2, of which 0 were waited for; matrix products, arithmetic and copies ran while one was open for 2% of the time, Pallas kernels for 0%

profile of v4, /device:TPU:0, one launch (start us, length us, event | category | flops | bytes accessed | tf_op | source)
XLA Modules:
  0.0 142.8 jit_solution(10628202381079731575)
XLA Ops:
  0.7 0.8 fusion.105
  1.6 1.2 convert_convert_fusion.1
  7.5 2.1 %fusion.14 = f32[1,2,1536]{2,0,1:T(1,128)S(1)} fusion(bf16[256,2,1536]{2,1,0:T(2,128)(2,1)} %param.21, f32[1,128]{1,0:T(1,128)S(1)} %get-tuple-element.49, f32[1,128]{1,0:T(1,128)S(1)} %get-tuple-element.50), kind=kOutput, calls=%fused_computation.20 | convolution fusion | flops 9437440 | bytes 1586176 | tf_op jit(solution)/shard_map/f,fjd->jd/dot_general | solution.py:301
  9.7 1.9 %all_gather.17 = f32[2,3072]{1,0:T(2,128)S(1)} all-gather(f32[2,1536]{1,0:T(2,128)S(1)} %bitcast.145), channel_id=1, replica_groups=mesh['group'=2,'seq'=8,'mp'=2] {'mp'}, dimensions={1}, use_global_device_ids=true | all-gather | bytes 36864 | tf_op jit(solution)/shard_map/all_gather | solution.py:307
  11.9 2.1 %all_gather.16 = bf16[64,3072]{1,0:T(8,128)(2,1)S(1)} all-gather(bf16[64,1536]{1,0:T(8,128)(2,1)S(1)} %copy-done.8), channel_id=1, replica_groups=mesh['group'=2,'seq'=8,'mp'=2] {'mp'}, dimensions={1}, use_global_device_ids=true | all-gather | bytes 589824 | tf_op jit(solution)/shard_map/all_gather | solution.py:300
  15.7 1.0 constant_dynamic-slice_fusion.1
  17.1 2.1 %all_gather.15 = bf16[2,384,256]{2,1,0:T(8,128)(2,1)S(1)} all-gather(bf16[1,384,256]{2,1,0:T(8,128)(2,1)S(1)} %copy.38), channel_id=1, replica_groups=mesh['group'=2,'seq'=8,'mp'=2] {'mp'}, dimensions={0}, use_global_device_ids=true | all-gather | bytes 589824 | tf_op jit(solution)/shard_map/all_gather | solution.py:319
  19.2 2.2 %fusion.5 = bf16[3072,256]{0,1:T(8,128)(2,1)} fusion(bf16[3072,384]{1,0:T(8,128)(2,1)S(1)} %copy-done, bf16[2,384,256]{2,1,0:T(8,128)(2,1)S(1)} %all_gather.15, s32[]{:T(128)S(6)} %select_n.40), kind=kOutput, calls=%fused_computation.9 | convolution fusion | flops 604766208 | bytes 4128772 | tf_op jit(solution)/shard_map/dot_general | solution.py:321
  21.4 2.6 %copy.39 = bf16[3072,256]{1,0:T(8,128)(2,1)} copy(bf16[3072,256]{0,1:T(8,128)(2,1)} %fusion.5) | data formatting | bytes 3145728 | tf_op jit(solution)/shard_map/convert_element_type | solution.py:321
  24.2 2.4 %copy.40 = bf16[384,1,1536]{0,2,1:T(8,128)(2,1)} copy(bf16[384,1,1536]{2,0,1:T(8,128)(2,1)} %param.16) | data formatting | bytes 2359296 | tf_op args[2]
  26.6 2.3 %fusion.95 = f32[2,12,128]{2,0,1:T(2,128)S(1)} fusion(bf16[12,128,384]{2,1,0:T(8,128)(2,1)} %bitcast.137, f32[2,384]{1,0:T(2,128)S(1)} %copy-done.36), kind=kOutput, calls=%fused_computation.142 | convolution fusion | flops 14155776 | bytes 1195008 | tf_op jit(solution)/shard_map/sk,kjd->sjd/dot_general | solution.py:336
  29.1 2.3 %convolution_convert_fusion.1.slim_ref = bf16[80,3072]{1,0:T(8,128)(2,1)S(1)} fusion(bf16[384,3072]{1,0:T(8,128)(2,1)} %param.22, bf16[65,384]{1,0:T(8,128)(2,1)S(1)} %fusion.88), kind=kOutput, calls=%fused_computation.11 | convolution fusion | flops 188989440 | bytes 2900736 | tf_op jit(solution)/shard_map/dot_general | solution.py:331
  31.5 67.9 %shard_map.157 = (bf16[2,4,384,256]{3,2,1,0:T(8,128)(2,1)S(1)}, bf16[80,3072]{1,0:T(8,128)(2,1)S(1)}, f32[2,12,128]{2,1,0:T(8,128)S(1)}, f32[2,128]{1,0:T(2,128)S(1)}, f32[4,64,128]{2,1,0:T(8,128)S(1)}) custom-call(bf16[2,4,384,256]{3,2,1,0:T(8,128)(2,1)S(1)} %bitcast.134, bf16[80,3072]{1,0:T(8,128)(2,1)S(1)} %convolution_convert_fusion.1.slim_ref, ...), custom_call_target="tpu_custom_call" | custom-call | tf_op jit(solution)/shard_map/pallas_call | solution.py:203
  99.4 1.2 copy-done.2
  101.0 3.4 %psum.14 = bf16[128,64]{0,1:T(8,128)(2,1)S(1)} all-reduce(bf16[128,64]{0,1:T(8,128)(2,1)S(1)} %convolution_convert_fusion.2), channel_id=1, replica_groups=mesh['group'=2,'seq'=8,'mp'=2] {'mp'}, use_global_device_ids=true, to_apply=%region_6.7 | all-reduce | flops 8192 | bytes 32768 | tf_op jit(solution)/shard_map/psum | solution.py:349
  104.9 1.3 collective-permute-start.1
  106.2 4.5 %collective-permute-start = (bf16[128,64]{0,1:T(8,128)(2,1)S(1)}, bf16[128,64]{0,1:T(8,128)(2,1)S(1)}, u32[]{:S(2)}, u32[]{:S(2)}) collective-permute-start(bf16[128,64]{0,1:T(8,128)(2,1)S(1)} %fusion.94), channel_id=1, source_target_pairs={{0,2},{2,4},{4,6},{6,8},{8,10},{10,12},{12,14},{1,3},{3,5},{5,7},{... | collective-permute-start | bytes 49160 | tf_op jit(solution)/shard_map/ppermute | solution.py:359
  110.8 1.7 %fusion.26 = f32[64,64]{1,0:T(8,128)S(1)} fusion(bf16[64,3072]{1,0:T(8,128)(2,1)S(1)} %all_gather.16, f32[64]{0:T(128)} %copy-done.46), kind=kOutput, calls=%fused_computation.38 | convolution fusion | flops 151388160 | bytes 409856 | tf_op jit(solution)/shard_map/cd,ed->ce/dot_general | solution.py:324
  114.4 0.9 multiply_reduce_fusion.2
  115.9 0.8 multiply_add_fusion.1
  117.3 1.6 %fusion.18 = bf16[384,256]{1,0:T(8,128)(2,1)S(1)} fusion(bf16[3072,256]{1,0:T(8,128)(2,1)S(1)} %bitcast.136, f32[384,3072]{1,0:T(8,128)S(1)} %multiply_add_fusion.1), kind=kOutput, calls=%fused_computation.25 | convolution fusion | flops 614694912 | bytes 6488064 | tf_op jit(solution)/shard_map/dot_general | solution.py:369
  119.0 2.3 %all-gather = bf16[768,256]{1,0:T(8,128)(2,1)S(1)} all-gather(bf16[384,256]{1,0:T(8,128)(2,1)S(1)} %fusion.18), channel_id=2, replica_groups=mesh['group'=2,'seq'=8,'mp'=2] {'mp'}, dimensions={0}, use_global_device_ids=true | all-gather | bytes 589824 | tf_op jit(solution)/shard_map/all_gather | solution.py:370
  122.1 1.1 copy.42
  123.2 1.5 %fusion.16 = f32[4,384,128]{1,2,0:T(8,128)} fusion(f32[4,64,128]{2,1,0:T(8,128)S(1)} %get-tuple-element.10, f32[384,128]{0,1:T(8,128)S(1)} %copy.43, f32[4]{0:T(128)S(1)} %convert_element_type.156, f32[384,128]{0,1:T(8,128)S(1)} %copy.42, f32[4]{0:T(128)S(1)} %convert_element_type.151, bf16[128,64]{0,1:T(8,128)(2,1)S(1)} %collective-permute-done.1, ...), kind=kOutput, calls=%fused_computation.23 | convolution fusion | flops 151928832 | bytes 1359904 | tf_op jit(solution)/shard_map/tc,kch->kth/dot_general | solution.py:371
  124.7 2.3 %copy.44 = f32[4,384,128]{2,1,0:T(8,128)} copy(f32[4,384,128]{1,2,0:T(8,128)} %fusion.16) | data formatting | bytes 1572864 | tf_op jit(solution)/shard_map/add | solution.py:372
  127.0 1.3 broadcast_multiply_fusion
  129.8 0.8 fusion.77
  130.6 1.3 reshape.200
  132.7 1.6 %multiply_reduce_fusion.1 = (bf16[2,64,128]{2,1,0:T(8,128)(2,1)}, bf16[2,64,128]{2,1,0:T(8,128)(2,1)}, bf16[4,2,64,128]{3,2,1,0:T(8,128)(2,1)}) fusion(bf16[4]{0:T(256)(128)(2,1)S(1)} %copy-done.37, bf16[4]{0:T(256)(128)(2,1)S(1)} %copy-done.38, f32[4,128]{1,0:T(4,128)S(1)} %copy-done.28, f32[4,4,64,128]{3,2,1,0:T(8,128)S(1)} %get-tuple-element.20, ...), kind=kLoop, calls=%fused_computation.119 | loop fusion | flops 1409024 | bytes 2033680 | tf_op jit(solution)/shard_map/reduce_sum | solution.py:392
  134.3 3.3 %fusion.17 = f32[128,64]{0,1:T(8,128)S(1)} fusion(bf16[3072,256]{1,0:T(8,128)(2,1)} %bitcast.135, f32[384,3072]{1,0:T(8,128)} %copy-done.4, bf16[80,3072]{1,0:T(8,128)(2,1)S(1)} %get-tuple-element.11, bf16[128,128]{1,0:T(8,128)(2,1)} %bitcast.149, bf16[128,128]{1,0:T(8,128)(2,1)} %bitcast.148), kind=kOutput, calls=%fused_computation.24 | convolution fusion | flops 259260416 | bytes 3637248 | tf_op jit(solution)/shard_map/dot_general | solution.py:403
  137.6 3.4 %psum.15 = f32[128,64]{0,1:T(8,128)S(1)} all-reduce(f32[128,64]{0,1:T(8,128)S(1)} %fusion.17), channel_id=1, replica_groups=mesh['group'=2,'seq'=8,'mp'=2] {'mp'}, use_global_device_ids=true, to_apply=%region_12.13 | all-reduce | flops 8192 | bytes 65536 | tf_op jit(solution)/shard_map/psum | solution.py:402
  141.1 1.6 %fusion.23 = f32[1,128,64]{1,2,0:T(8,128)} fusion(bf16[4,128,128]{2,1,0:T(8,128)(2,1)S(1)} %bitcast.141, f32[4,64,128]{2,1,0:T(8,128)S(1)} %get-tuple-element.10, f32[128,64]{0,1:T(8,128)S(1)} %psum.15, f32[384,64]{0,1:T(8,128)} %get-tuple-element.46, f32[128]{0:T(128)S(1)} %copy-done.44, f32[128]{0:T(128)S(1)} %broadcast_multiply_fusion.1, ...), kind=kOutput, calls=%fused_computation.30 | convolution fusion | flops 50380800 | bytes 361988 | tf_op jit(solution)/shard_map/kth,kch->tc/dot_general | solution.py:389
  (141 shorter events, 10.1 us)
Async XLA Ops:
  0.6 18.6 %copy-start = (bf16[3072,384]{1,0:T(8,128)(2,1)S(1)}, bf16[3072,384]{1,0:T(8,128)(2,1)}, u32[]{:S(2)}) copy-start(bf16[3072,384]{1,0:T(8,128)(2,1)} %param.23) | copy-start | bytes 7077892
  0.6 11.0 %copy-start.6 = (bf16[1,128,1536]{2,1,0:T(8,128)(2,1)S(1)}, bf16[1,128,1536]{2,1,0:T(8,128)(2,1)}, u32[]{:S(2)}) copy-start(bf16[1,128,1536]{2,1,0:T(8,128)(2,1)} %param.14) | copy-start | bytes 1179652
  0.7 11.3 %copy-start.8 = (bf16[64,1536]{1,0:T(8,128)(2,1)S(1)}, bf16[64,1536]{1,0:T(8,128)(2,1)}, u32[]{:S(2)}) copy-start(bf16[64,1536]{1,0:T(8,128)(2,1)} %param.20) | copy-start | bytes 589828
  2.9 1.2 copy-start.41
  6.7 7.4 %copy-start.5 = (bf16[4,1536,128]{2,1,0:T(8,128)(2,1)S(1)}, bf16[4,1536,128]{2,1,0:T(8,128)(2,1)}, u32[]{:S(2)}) copy-start(bf16[4,1536,128]{2,1,0:T(8,128)(2,1)} %param.24) | copy-start | bytes 4718596
  24.0 2.6 %copy-start.36 = (f32[2,384]{1,0:T(2,128)S(1)}, f32[2,384]{1,0:T(2,128)}, u32[]{:S(2)}) copy-start(f32[2,384]{1,0:T(2,128)} %param.15) | copy-start | bytes 9220
  24.2 4.7 %copy-start.46 = (f32[64]{0:T(128)}, f32[64]{0:T(128)S(1)}, u32[]{:S(2)}) copy-start(f32[64]{0:T(128)S(1)} %broadcast_multiply_fusion.2) | copy-start | bytes 772
  29.0 2.4 %copy-start.1 = (bf16[3072,256]{1,0:T(8,128)(2,1)S(1)}, bf16[3072,256]{1,0:T(8,128)(2,1)}, u32[]{:S(2)}) copy-start(bf16[3072,256]{1,0:T(8,128)(2,1)} %copy.39) | copy-start | bytes 4718596
  31.4 69.2 %copy-start.7 = (bf16[1,128,1536]{2,1,0:T(8,128)(2,1)S(1)}, bf16[1,128,1536]{2,1,0:T(8,128)(2,1)}, u32[]{:S(2)}) copy-start(bf16[1,128,1536]{2,1,0:T(8,128)(2,1)} %param.14) | copy-start | bytes 1179652
  31.4 69.2 %copy-start.47 = (bf16[1536,64]{0,1:T(8,128)(2,1)S(1)}, bf16[1536,64]{0,1:T(8,128)(2,1)}, u32[]{:S(2)}) copy-start(bf16[1536,64]{0,1:T(8,128)(2,1)} %param.17) | copy-start | bytes 589828
  31.5 72.9 %copy-start.32 = (bf16[1,128,64]{1,2,0:T(8,128)(2,1)S(1)}, bf16[1,128,64]{1,2,0:T(8,128)(2,1)}, u32[]{:S(2)}) copy-start(bf16[1,128,64]{1,2,0:T(8,128)(2,1)} %param.19) | copy-start | bytes 49156
  99.3 1.2 copy-start.2
  100.5 12.6 %copy-start.31 = (f32[4,3,3,128]{3,0,2,1:T(4,128)S(1)}, f32[4,3,3,128]{3,0,2,1:T(4,128)}, u32[]{:S(2)}) copy-start(f32[4,3,3,128]{3,0,2,1:T(4,128)} %param.25) | copy-start | bytes 55300
  100.5 13.3 %copy-start.42 = (pred[4]{0:T(512)(128)(4,1)S(1)}, pred[4]{0:T(512)(128)(4,1)}, u32[]{:S(2)}) copy-start(pred[4]{0:T(512)(128)(4,1)} %copy-done.41) | copy-start | bytes 16
  100.5 13.3 %copy-start.40 = (pred[4]{0:T(512)(128)(4,1)S(1)}, pred[4]{0:T(512)(128)(4,1)}, u32[]{:S(2)}) copy-start(pred[4]{0:T(512)(128)(4,1)} %copy-done.39) | copy-start | bytes 16
  100.5 13.3 %copy-start.34 = (f32[4,128]{1,0:T(4,128)S(1)}, f32[4,128]{1,0:T(4,128)}, u32[]{:S(2)}) copy-start(f32[4,128]{1,0:T(4,128)} %param.26) | copy-start | bytes 6148
  104.9 9.5 %collective-permute-start.1 = (bf16[128,64]{0,1:T(8,128)(2,1)S(1)}, bf16[128,64]{0,1:T(8,128)(2,1)S(1)}, u32[]{:S(2)}, u32[]{:S(2)}) collective-permute-start(bf16[128,64]{0,1:T(8,128)(2,1)S(1)} %fusion.94), channel_id=1, source_target_pairs={{2,0},{4,2},{6,4},{8,6},{10,8},{12,10},{14,12},{3,1},{5,3},{7,5},{... | collective-permute-start | bytes 49160 | tf_op jit(solution)/shard_map/ppermute | solution.py:360
  106.2 8.2 %collective-permute-start = (bf16[128,64]{0,1:T(8,128)(2,1)S(1)}, bf16[128,64]{0,1:T(8,128)(2,1)S(1)}, u32[]{:S(2)}, u32[]{:S(2)}) collective-permute-start(bf16[128,64]{0,1:T(8,128)(2,1)S(1)} %fusion.94), channel_id=1, source_target_pairs={{0,2},{2,4},{4,6},{6,8},{8,10},{10,12},{12,14},{1,3},{3,5},{5,7},{... | collective-permute-start | bytes 49160 | tf_op jit(solution)/shard_map/ppermute | solution.py:359
  114.4 2.3 %copy-start.10 = (bf16[128,64]{0,1:T(8,128)(2,1)}, bf16[128,64]{0,1:T(8,128)(2,1)S(1)}, u32[]{:S(2)}) copy-start(bf16[128,64]{0,1:T(8,128)(2,1)S(1)} %collective-permute-done) | copy-start | bytes 49156
  115.9 1.4 copy-start.3
  116.8 2.2 %copy-start.4 = (f32[384,3072]{1,0:T(8,128)}, f32[384,3072]{1,0:T(8,128)S(1)}, u32[]{:S(2)}) copy-start(f32[384,3072]{1,0:T(8,128)S(1)} %multiply_add_fusion.1) | copy-start | bytes 14155780
  119.0 4.2 %copy-start.11 = (bf16[128,64]{0,1:T(8,128)(2,1)S(1)}, bf16[128,64]{0,1:T(8,128)(2,1)}, u32[]{:S(2)}) copy-start(bf16[128,64]{0,1:T(8,128)(2,1)} %copy-done.10) | copy-start | bytes 49156
  128.3 0.7 copy-start.17
  128.4 0.7 copy-start.29
  128.4 0.7 copy-start.33
  129.0 0.8 copy-start.35
  132.0 0.7 copy-start.18
  132.0 0.7 copy-start.20
  132.0 0.7 copy-start.22
  134.3 6.8 %copy-start.9 = (bf16[4,2,64,128]{3,2,1,0:T(8,128)(2,1)S(1)}, bf16[4,2,64,128]{3,2,1,0:T(8,128)(2,1)}, u32[]{:S(2)}) copy-start(bf16[4,2,64,128]{3,2,1,0:T(8,128)(2,1)} %get-tuple-element.15) | copy-start | bytes 393220
  134.3 6.8 %copy-start.43 = (f32[128]{0:T(128)S(1)}, f32[128]{0:T(128)}, u32[]{:S(2)}) copy-start(f32[128]{0:T(128)} %get-tuple-element.41) | copy-start | bytes 1540
  134.3 6.8 %copy-start.44 = (f32[128]{0:T(128)S(1)}, f32[128]{0:T(128)}, u32[]{:S(2)}) copy-start(f32[128]{0:T(128)} %get-tuple-element.42) | copy-start | bytes 1540
  (18 other events, 11.9 us)
